TPU v7x, 32 devices: a whole 2x2x4 slice. The times are simulated.
32 devices in a mesh: region: 8 (over y, x, core), local: 4 (over z).
Axes of the slice: x: 2, y: 2, z: 4, core: 2. Of those that a mesh axis runs over, the one named last changes fastest.
Arguments:
- tokens: bfloat16 [1024, 7168], P('region', 'local'), may hold values from -44 to 44
- norm_gain: float32 [7168], P('local'), may hold values from 0.1 to 1.9
- w_gate: bfloat16 [8, 7168, 2048], P('region', None, 'local'), may hold values from -0.0625 to 0.0625
- w_up: bfloat16 [8, 7168, 2048], P('region', None, 'local'), may hold values from -0.0625 to 0.0625
- w_down: bfloat16 [8, 2048, 7168], P('region', 'local'), may hold values from -0.125 to 0.125
- regions: int32 [1024, 2], P('region'), may hold values from 0 to 7, all different within a row; in each aligned block of 128 rows (0 to 127, 128 to 255, ...) at most 40 rows name the same one
- combine: float32 [1024, 2], P('region'), may hold values from 0.1 to 1
- grad_out: bfloat16 [1024, 7168], P('region', 'local'), may hold values from -3 to 3
Outputs:
- moe_out: bfloat16 [1024, 7168], P('region', 'local')
- grad_tokens: bfloat16 [1024, 7168], P('region', 'local')
- grad_combine: float32 [1024, 2], P('region')
Inputs may be any that keep to these rules, and one draw needn't show every extreme that they name: `regions`: each row names 2 different experts; among the rows of one device (aligned blocks of 128 rows) no expert is named by more than 40 rows, a bound that some block reaches.
All inputs are finite; a program needn't handle non-finite values.
Results may differ from a plain program's by a relative error of at most 0.02.
Values may be sent and summed in bfloat16 or wider, within the bound.
A program may use at most 128 MiB of HBM per device.

v0:
```python
import jax
import jax.numpy as jnp
from jax import lax
from jax.sharding import PartitionSpec as P

D = 7168


def on_device(tokens, norm_gain, w_gate, w_up, w_down, regions, combine, grad_out):
    inputs_f32 = tokens.astype(jnp.float32)
    token_count, width_local = inputs_f32.shape
    region_count = lax.axis_size("region")
    route_count = regions.shape[1]
    capacity = max(2, token_count * route_count * 5 // (4 * region_count))
    slot_total = region_count * capacity
    sum_squares = lax.psum(jnp.sum(inputs_f32 * inputs_f32, axis=1), "local")
    inv_rms = lax.rsqrt(sum_squares / D + 1e-06)[:, None]
    normed = (inputs_f32 * inv_rms * norm_gain).astype(jnp.bfloat16)
    flat_routes = regions.reshape(-1)
    one_hot = (flat_routes[:, None] == jnp.arange(region_count, dtype=jnp.int32)[None, :]).astype(
        jnp.int32
    )
    running = jnp.cumsum(one_hot, axis=0) - one_hot
    slot_index = jnp.sum(running * one_hot, axis=1)
    placement = flat_routes * capacity + slot_index
    owner = jnp.arange(token_count * route_count, dtype=jnp.int32) // route_count
    source = jnp.full((slot_total,), token_count, jnp.int32).at[placement].set(owner)

    def pack_rows(matrix):
        picked = jnp.take(matrix, source, axis=0, mode="fill", fill_value=0)
        return picked.reshape(region_count, capacity, matrix.shape[1])

    gate_w = w_gate[0]
    up_w = w_up[0]
    down_w = w_down[0]
    contract_last = (((1,), (1,)), ((), ()))
    normed_full, grad_full = (
        lax.all_gather(normed, "local", axis=1, tiled=True),
        lax.all_gather(grad_out, "local", axis=1, tiled=True),
    )
    sent_in, sent_grad = (
        lax.all_to_all(pack_rows(normed_full), "region", split_axis=0, concat_axis=0, tiled=True),
        lax.all_to_all(pack_rows(grad_full), "region", split_axis=0, concat_axis=0, tiled=True),
    )
    rows_in = sent_in.reshape(slot_total, D)
    rows_grad = sent_grad.reshape(slot_total, D)
    gate_pre = jnp.dot(rows_in, gate_w, preferred_element_type=jnp.float32)
    up_pre = jnp.dot(rows_in, up_w, preferred_element_type=jnp.float32)
    grad_hidden = lax.dot_general(
        rows_grad, down_w, contract_last, preferred_element_type=jnp.float32
    )
    sig_gate = jax.nn.sigmoid(gate_pre)
    act_gate = gate_pre * sig_gate
    hidden = (act_gate * up_pre).astype(jnp.bfloat16)
    grad_gate = (grad_hidden * up_pre * sig_gate * (1.0 + gate_pre * (1.0 - sig_gate))).astype(
        jnp.bfloat16
    )
    grad_up = (grad_hidden * act_gate).astype(jnp.bfloat16)
    expert_out = jnp.dot(hidden, down_w, preferred_element_type=jnp.float32)
    stacked_grads = jnp.concatenate((grad_gate, grad_up), axis=1)
    stacked_weights = jnp.concatenate((gate_w, up_w), axis=1)
    branch_grad = lax.dot_general(
        stacked_grads, stacked_weights, contract_last, preferred_element_type=jnp.float32
    )
    out_share, grad_share = (
        lax.psum_scatter(
            expert_out.astype(jnp.bfloat16), "local", scatter_dimension=1, tiled=True
        ).astype(jnp.float32),
        lax.psum_scatter(
            branch_grad.astype(jnp.bfloat16), "local", scatter_dimension=1, tiled=True
        ).astype(jnp.float32),
    )
    back_out, back_grad = (
        lax.all_to_all(
            out_share.reshape(region_count, capacity, width_local).astype(jnp.bfloat16),
            "region",
            split_axis=0,
            concat_axis=0,
            tiled=True,
        ).astype(jnp.float32),
        lax.all_to_all(
            grad_share.reshape(region_count, capacity, width_local).astype(jnp.bfloat16),
            "region",
            split_axis=0,
            concat_axis=0,
            tiled=True,
        ).astype(jnp.float32),
    )
    pick_index = placement.reshape(token_count, route_count)
    out_picked = back_out.reshape(slot_total, width_local)[pick_index]
    grad_picked = back_grad.reshape(slot_total, width_local)[pick_index]
    weights = combine[:, :, None]
    moe_out = jnp.sum(weights * out_picked, axis=1).astype(jnp.bfloat16)
    grad_normed = jnp.sum(weights * grad_picked, axis=1)
    scaled = norm_gain * grad_normed
    inner_part = jnp.sum(inputs_f32 * scaled, axis=1)
    comb_part = jnp.sum(grad_out.astype(jnp.float32)[:, None, :] * out_picked, axis=2)
    inner, grad_combine = lax.psum((inner_part, comb_part), "local")
    grad_tokens = (
        inv_rms * scaled - inputs_f32 * inv_rms * inv_rms * inv_rms * inner[:, None] / D
    ).astype(jnp.bfloat16)
    return (moe_out, grad_tokens, grad_combine)


def solution(mesh):
    placed = (
        P("region", "local"),
        P("local"),
        P("region", None, "local"),
        P("region", None, "local"),
        P("region", "local", None),
        P("region", None),
        P("region", None),
        P("region", "local"),
    )
    return jax.shard_map(
        on_device,
        mesh=mesh,
        in_specs=placed,
        out_specs=(P("region", "local"), P("region", "local"), P("region", None)),
        check_vma=False,
    )
```

profile of v0, /device:TPU:0, one launch (start us, length us, event | category | flops | bytes accessed | tf_op | source)
XLA Modules:
  0.0 495.0 jit_solution(5279378590460265649)
XLA Ops:
  7.2 1.2 fusion.18
  8.4 13.5 %psum.21 = f32[128]{0:T(128)S(1)} all-reduce(f32[128]{0:T(128)S(1)} %fusion.18), channel_id=1, replica_groups=mesh['region'=8,'local'=4] {'local'}, use_global_device_ids=true, to_apply=%region_1.0 | all-reduce | flops 128 | bytes 1024 | tf_op jit(solution)/shard_map/psum | solution.py:16
  21.9 2.0 fusion.12
  23.9 0.0 all-gather.5.cloned.1.call-start
  23.9 0.7 all-gather.5.cloned.1.call-update
  24.6 0.8 copy.17
  25.4 0.1 eq.29
  25.5 0.1 eq.25
  25.7 0.6 reduce-window.6
  26.3 0.2 slice_reduce_fusion
  26.5 0.1 fusion.26
  26.6 0.1 reduce_sum.61
  26.8 0.1 mul.129
  27.0 1.4 scatter_custom_fusion
  28.4 35.2 %all-gather.3.cloned.1.call-done = bf16[128,7168]{1,0:T(8,128)(2,1)} async-done(((bf16[128,1792]{1,0:T(8,128)(2,1)}), bf16[128,7168]{1,0:T(8,128)(2,1)}) %all-gather.3.cloned.1.call-update) | async-done | bytes 1835024 | tf_op jit(solution)/shard_map/all_gather | solution.py:38
  63.6 14.6 %gather_fusion.2 = bf16[320,7168]{1,0:T(8,128)(2,1)} fusion(bf16[128,7168]{1,0:T(8,128)(2,1)} %all-gather.3.cloned.1.call-done, s32[1024]{0:T(1024)S(1)} %pad_clamp_fusion.1), kind=kCustom, calls=%fused_computation.clone | custom fusion | bytes 9176320 | tf_op jit(solution)/shard_map/jit(_take)/gather | solution.py:30
  78.2 27.2 %all-gather.5.cloned.1.call-done = bf16[128,7168]{1,0:T(8,128)(2,1)} async-done(((bf16[128,1792]{1,0:T(8,128)(2,1)}), bf16[128,7168]{1,0:T(8,128)(2,1)}) %all-gather.5.cloned.1.call-update) | async-done | bytes 1835024 | tf_op jit(solution)/shard_map/all_gather | solution.py:39
  105.5 14.9 %gather_fusion.3 = bf16[320,7168]{1,0:T(8,128)(2,1)} fusion(bf16[128,7168]{1,0:T(8,128)(2,1)} %all-gather.5.cloned.1.call-done, s32[1024]{0:T(1024)S(1)} %pad_clamp_fusion.1), kind=kCustom, calls=%fused_computation.1.clone | custom fusion | bytes 9176320 | tf_op jit(solution)/shard_map/jit(_take)/gather | solution.py:30
  120.4 6.5 %broadcast_select_fusion = (bf16[320,7168]{1,0:T(8,128)(2,1)}, bf16[320,7168]{1,0:T(8,128)(2,1)S(1)}) fusion(bf16[320,7168]{1,0:T(8,128)(2,1)} %gather_fusion.3, pred[320]{0:T(512)(128)(4,1)S(1)} %compare_and_fusion, bf16[320,7168]{1,0:T(8,128)(2,1)} %gather_fusion.2), kind=kLoop, calls=%fused_computation.14 | loop fusion | flops 4587520 | bytes 18350400 | tf_op jit(solution)/shard_map/jit(_take)/select_n | solution.py:30
  126.9 56.8 %all_to_all.20 = bf16[8,40,7168]{2,1,0:T(8,128)(2,1)} all-to-all(bf16[8,40,7168]{2,1,0:T(8,128)(2,1)S(1)} %bitcast.39), channel_id=1, replica_groups=mesh['region'=8,'local'=4] {'region'}, dimensions={0} | all-to-all | bytes 9175040 | tf_op jit(solution)/shard_map/all_to_all | solution.py:42
  183.7 4.6 all-to-all-start.2
  188.3 0.3 reduce-scatter.5.cloned.1.call-start
  188.6 7.0 %fusion.31 = f32[320,512]{1,0:T(8,128)S(1)} fusion(bf16[320,7168]{1,0:T(8,128)(2,1)} %bitcast.40, bf16[1,7168,512]{2,1,0:T(8,128)(2,1)} %param.13), kind=kOutput, calls=%fused_computation.64 | convolution fusion | flops 2348810240 | bytes 12582912 | tf_op jit(solution)/shard_map/dot_general | solution.py:48
  195.6 46.1 %all-to-all-done.2 = bf16[8,40,7168]{2,1,0:T(8,128)(2,1)} async-done(((bf16[8,40,7168]{2,1,0:T(8,128)(2,1)}), bf16[8,40,7168]{2,1,0:T(8,128)(2,1)}, u32[]{:S(2)}, u32[]{:S(2)}) %all-to-all-start.2) | async-done | bytes 4587552 | tf_op jit(solution)/shard_map/all_to_all | solution.py:43
  241.7 7.2 %fusion.7 = f32[320,512]{1,0:T(8,128)S(1)} fusion(bf16[320,7168]{1,0:T(8,128)(2,1)} %bitcast.12, bf16[1,512,7168]{2,1,0:T(8,128)(2,1)} %param.14), kind=kOutput, calls=%fused_computation.11 | convolution fusion | flops 2348810240 | bytes 12582912 | tf_op jit(solution)/shard_map/dot_general | solution.py:49
  248.9 5.9 %multiply_convert_fusion.1 = (bf16[320,512]{1,0:T(8,128)(2,1)S(1)}, bf16[320,512]{1,0:T(8,128)(2,1)S(1)}, f32[320,512]{1,0:T(8,128)S(1)}) fusion(f32[320,512]{1,0:T(8,128)S(1)} %fusion.7, f32[320,512]{1,0:T(8,128)S(1)} %fusion.31, bf16[320,7168]{1,0:T(8,128)(2,1)S(1)} %bitcast.41, bf16[1,7168,512]{2,1,0:T(8,128)(2,1)} %param.12), kind=kOutput, calls=%fused_computation.38 | convolution fusion | flops 2350940160 | bytes 14548992 | tf_op jit(solution)/shard_map/dot_general | solution.py:47
  254.8 9.7 %fusion.4 = bf16[320,7168]{1,0:T(8,128)(2,1)} fusion(bf16[7168,512]{1,0:T(8,128)(2,1)} %bitcast.46, bf16[7168,512]{1,0:T(8,128)(2,1)} %bitcast.47, bf16[320,512]{1,0:T(8,128)(2,1)S(1)} %get-tuple-element.13, bf16[320,512]{1,0:T(8,128)(2,1)S(1)} %get-tuple-element.12), kind=kOutput, calls=%fused_computation.9 | convolution fusion | flops 4730585088 | bytes 19922944 | tf_op jit(solution)/shard_map/dot_general | solution.py:62
  264.6 0.0 reduce-scatter.3.cloned.1.call-start
  264.6 7.8 %convolution_convert_fusion = bf16[320,7168]{1,0:T(8,128)(2,1)} fusion(bf16[1,512,7168]{2,1,0:T(8,128)(2,1)} %param.14, f32[320,512]{1,0:T(8,128)S(1)} %fusion.31, f32[320,512]{1,0:T(8,128)S(1)} %get-tuple-element.18), kind=kOutput, calls=%fused_computation.10 | convolution fusion | flops 2352087040 | bytes 13238272 | tf_op jit(solution)/shard_map/dot_general | solution.py:59
  272.5 72.5 %reduce-scatter.5.cloned.1.call-done = bf16[320,1792]{1,0:T(8,128)(2,1)} async-done(((bf16[320,7168]{1,0:T(8,128)(2,1)}), bf16[320,1792]{1,0:T(8,128)(2,1)}) %reduce-scatter.5.cloned.1.call-update) | async-done | bytes 1146896 | tf_op jit(solution)/shard_map/reduce_scatter | solution.py:69
  344.9 3.6 all-to-all-start.3
  348.6 82.2 %reduce-scatter.3.cloned.1.call-done = bf16[320,1792]{1,0:T(8,128)(2,1)} async-done(((bf16[320,7168]{1,0:T(8,128)(2,1)}), bf16[320,1792]{1,0:T(8,128)(2,1)}) %reduce-scatter.3.cloned.1.call-update) | async-done | bytes 1146896 | tf_op jit(solution)/shard_map/reduce_scatter | solution.py:66
  430.8 4.5 all-to-all-start.1
  435.3 1.0 convert_element_type.62
  436.3 0.1 reshape.123
  436.5 0.1 copy.16
  436.6 0.2 bitcast_convert_fusion
  436.8 2.6 gather_fusion.1
  439.5 3.3 reshape.130
  442.8 8.8 %all-to-all-done.1 = bf16[8,40,1792]{2,1,0:T(8,128)(2,1)} async-done(((bf16[8,40,1792]{2,1,0:T(8,128)(2,1)}), bf16[8,40,1792]{2,1,0:T(8,128)(2,1)}, u32[]{:S(2)}, u32[]{:S(2)}) %all-to-all-start.1) | async-done | bytes 1146912 | tf_op jit(solution)/shard_map/all_to_all | solution.py:74
  451.5 1.4 bitcast_convert_fusion.1
  452.9 2.6 gather_fusion
  455.6 3.4 reshape.122
  459.0 8.3 %multiply_reduce_fusion = (f32[128,2]{1,0:T(8,128)S(1)}, bf16[128,1792]{1,0:T(8,128)(2,1)}, f32[128,1792]{1,0:T(8,128)S(1)}) fusion(f32[128,2,1792]{2,1,0:T(2,128)} %reshape.122, f32[128,1792]{1,0:T(8,128)} %convert_element_type.62, f32[128,2]{1,0:T(8,128)S(1)} %copy.16, f32[128,2,1792]{2,1,0:T(2,128)S(1)} %copy-done), kind=kLoop, calls=%fused_computation.16 | loop fusion | flops 2293504 | bytes 5965824 | tf_op jit(solution)/shard_map/reduce_sum | solution.py:97
  467.3 0.2 fusion.19
  467.5 19.2 %all-reduce = (f32[128]{0:T(128)S(1)}, f32[128,2]{1,0:T(8,128)S(1)}) all-reduce(f32[128]{0:T(128)S(1)} %fusion.19, f32[128,2]{1,0:T(8,128)S(1)} %get-tuple-element.7), channel_id=1, replica_groups=mesh['region'=8,'local'=4] {'local'}, use_global_device_ids=true, to_apply=%region_11.13 | all-reduce | flops 384 | bytes 3072 | tf_op jit(solution)/shard_map/psum | solution.py:98
  486.7 1.1 fusion.17
  487.8 0.6 copy.20
  (28 shorter events, 0.2 us)
Async XLA Ops:
  7.2 56.5 %all-gather.3.cloned.1.call-start = ((), (), s32[]{:S(2)}) async-start(), calls=%async_computation.6 | async-start | bytes 2293760 | tf_op jit(solution)/shard_map/all_gather | solution.py:38
  23.9 81.6 %all-gather.5.cloned.1.call-start = ((), (), s32[]{:S(2)}) async-start(), calls=%async_computation.8 | async-start | bytes 2293760 | tf_op jit(solution)/shard_map/all_gather | solution.py:39
  183.7 57.9 %all-to-all-start.2 = ((bf16[8,40,7168]{2,1,0:T(8,128)(2,1)}), bf16[8,40,7168]{2,1,0:T(8,128)(2,1)}, u32[]{:S(2)}, u32[]{:S(2)}) async-start(bf16[8,40,7168]{2,1,0:T(8,128)(2,1)} %bitcast.38), calls=%async_computation.3 | async-start | bytes 9175040 | tf_op jit(solution)/shard_map/all_to_all | solution.py:43
  188.3 156.6 %reduce-scatter.5.cloned.1.call-start = ((), (), s32[]{:S(2)}) async-start(), calls=%async_computation.9 | async-start | bytes 5734400 | tf_op jit(solution)/shard_map/reduce_scatter | solution.py:69
  241.7 7.2 %copy-start.2 = (bf16[8,40,7168]{2,1,0:T(8,128)(2,1)S(1)}, bf16[8,40,7168]{2,1,0:T(8,128)(2,1)}, u32[]{:S(2)}) copy-start(bf16[8,40,7168]{2,1,0:T(8,128)(2,1)} %all_to_all.20) | copy-start | bytes 13762564
  264.6 166.2 %reduce-scatter.3.cloned.1.call-start = ((), (), s32[]{:S(2)}) async-start(), calls=%async_computation.7 | async-start | bytes 5734400 | tf_op jit(solution)/shard_map/reduce_scatter | solution.py:66
  272.4 162.9 %copy-start.3 = (bf16[128,1792]{1,0:T(8,128)(2,1)S(1)}, bf16[128,1792]{1,0:T(8,128)(2,1)}, u32[]{:S(2)}) copy-start(bf16[128,1792]{1,0:T(8,128)(2,1)} %param.17) | copy-start | bytes 1376260
  272.4 164.0 %copy-start.5 = (f32[128,2]{0,1:T(2,128)S(1)}, f32[128,2]{0,1:T(2,128)}, u32[]{:S(2)}) copy-start(f32[128,2]{0,1:T(2,128)} %param.16) | copy-start | bytes 3076
  344.9 85.9 %all-to-all-start.3 = ((bf16[8,40,1792]{2,1,0:T(8,128)(2,1)}), bf16[8,40,1792]{2,1,0:T(8,128)(2,1)S(1)}, u32[]{:S(2)}, u32[]{:S(2)}) async-start(bf16[8,40,1792]{2,1,0:T(8,128)(2,1)} %bitcast.43), calls=%async_computation.5 | async-start | bytes 2293760 | tf_op jit(solution)/shard_map/all_to_all | solution.py:81
  430.8 20.7 %all-to-all-start.1 = ((bf16[8,40,1792]{2,1,0:T(8,128)(2,1)}), bf16[8,40,1792]{2,1,0:T(8,128)(2,1)}, u32[]{:S(2)}, u32[]{:S(2)}) async-start(bf16[8,40,1792]{2,1,0:T(8,128)(2,1)} %bitcast.42), calls=%async_computation.2 | async-start | bytes 2293760 | tf_op jit(solution)/shard_map/all_to_all | solution.py:74
  455.6 3.4 copy-start
  455.6 11.7 %copy-start.1 = (bf16[128,1792]{1,0:T(8,128)(2,1)S(1)}, bf16[128,1792]{1,0:T(8,128)(2,1)}, u32[]{:S(2)}) copy-start(bf16[128,1792]{1,0:T(8,128)(2,1)} %param.10) | copy-start | bytes 1376260
  455.6 11.7 %copy-start.4 = (f32[1792]{0:T(1024)S(1)}, f32[1792]{0:T(1024)}, u32[]{:S(2)}) copy-start(f32[1792]{0:T(1024)} %param.11) | copy-start | bytes 21508
Sparse Core Ops, SparseCore 0:
  24.0 39.5 all-gather.2
  65.2 40.2 all-gather.4
  264.7 80.2 reduce-scatter.4
  347.1 83.6 reduce-scatter.2
where the time goes:
time: 496 us; the launch traced here: 495 us
  waiting for transfers between devices  273 us (55%)
  blocking collectives  89.5 us (18%)
  local copies, waits for them, and re-layouts  45.3 us (9%)
  matrix products  37.7 us (8%)
  other arithmetic  22.7 us (5%)
  between operations  13.9 us (3%)
  starting transfers between devices  13.1 us (3%)
    reduce_scatter x1, waiting for transfers between devices, on_device(): lax.psum_scatter(expert_out.astype(jnp.bfloat16), 'local', scatter_dimens...  82.2 us
    reduce_scatter x1, waiting for transfers between devices, on_device(): lax.psum_scatter(branch_grad.astype(jnp.bfloat16), 'local', scatter_dimen...  72.5 us
    all_to_all x1, blocking collectives, on_device(): lax.all_to_all(pack_rows(normed_full), 'region', split_axis=0, concat_axi...  56.8 us
    all_to_all x1, waiting for transfers between devices, on_device(): lax.all_to_all(pack_rows(grad_full), 'region', split_axis=0, concat_axis=...  46.1 us
    all_gather x1, waiting for transfers between devices, on_device(): lax.all_gather(normed, 'local', axis=1, tiled=True)  35.2 us
    gather x2, local copies, waits for them, and re-layouts, pack_rows(): picked = jnp.take(matrix, source, axis=0, mode='fill', fill_value=0)  29.5 us
    all_gather x1, waiting for transfers between devices, on_device(): lax.all_gather(grad_out, 'local', axis=1, tiled=True)  27.2 us
    psum x1, blocking collectives, on_device(): inner, grad_combine = lax.psum((inner_part, comb_part), 'local')  19.2 us
  transfers between devices with their start and end apart: 7, of which 6 were waited for; matrix products, arithmetic and copies ran while one was open for 8% of the time, Pallas kernels for 0%

commit v1 on v0

v1 whole, which is shorter than its diff:
```python
import jax
import jax.numpy as jnp
from jax import lax
from jax.sharding import PartitionSpec as P

D = 7168
F32 = jnp.float32
BF16 = jnp.bfloat16
LAST = (((1,), (1,)), ((), ()))


def dot(left, right):
    return jnp.dot(left, right, preferred_element_type=F32)


def split_weights(weights):
    high = weights.astype(BF16)
    return high, (weights - high.astype(F32)).astype(BF16)


def on_device(tokens, norm_gain, w_gate, w_up, w_down, regions, combine, grad_out):
    token_count, width_local = tokens.shape
    region_count = lax.axis_size("region")
    route_count = regions.shape[1]
    capacity = max(2, token_count * route_count * 5 // (4 * region_count))
    slot_total = region_count * capacity
    gate_w, up_w, down_w = w_gate[0], w_up[0], w_down[0]

    gain_full = lax.all_gather(norm_gain, "local", axis=0, tiled=True)
    tokens_full = lax.all_gather(tokens, "local", axis=1, tiled=True)
    grad_full = lax.all_gather(grad_out, "local", axis=1, tiled=True)

    flat_routes = regions.reshape(-1)
    one_hot = (flat_routes[:, None] == jnp.arange(region_count, dtype=jnp.int32)[None, :]).astype(F32)
    pairs = token_count * route_count
    earlier = (jnp.arange(pairs)[:, None] > jnp.arange(pairs)[None, :]).astype(F32)
    running = dot(earlier.astype(BF16), one_hot.astype(BF16))
    slot_index = jnp.sum(running * one_hot, axis=1).astype(jnp.int32)
    placement = (flat_routes * capacity + slot_index).reshape(token_count, route_count)
    hits = placement[:, :, None] == jnp.arange(slot_total, dtype=jnp.int32)[None, None, :]
    spread = jnp.sum(hits.astype(F32), axis=1).astype(BF16)
    weighted = jnp.sum(jnp.where(hits, combine[:, :, None], 0.0), axis=1)
    weight_high, weight_low = split_weights(weighted)

    def pack_rows(matrix):
        picked = lax.dot_general(spread, matrix, (((0,), (0,)), ((), ())), preferred_element_type=F32)
        return picked.astype(BF16).reshape(region_count, capacity, matrix.shape[1])

    def exchange(blocks):
        return lax.all_to_all(blocks, "region", split_axis=0, concat_axis=0, tiled=True)

    inputs_full = tokens_full.astype(F32)
    inv_rms = lax.rsqrt(jnp.sum(inputs_full * inputs_full, axis=1, keepdims=True) / D + 1e-06)
    normed = (inputs_full * inv_rms * gain_full).astype(BF16)
    rows_in = exchange(pack_rows(normed)).reshape(slot_total, D)
    rows_grad = exchange(pack_rows(grad_full)).reshape(slot_total, D)

    gate_pre = dot(rows_in, gate_w)
    up_pre = dot(rows_in, up_w)
    sig_gate = jax.nn.sigmoid(gate_pre)
    act_gate = gate_pre * sig_gate
    hidden = (act_gate * up_pre).astype(BF16)
    expert_out = dot(hidden, down_w).astype(BF16)
    grad_hidden = lax.dot_general(rows_grad, down_w, LAST, preferred_element_type=F32)
    grad_gate = (grad_hidden * up_pre * sig_gate * (1.0 + gate_pre * (1.0 - sig_gate))).astype(BF16)
    grad_up = (grad_hidden * act_gate).astype(BF16)
    branch_grad = (
        lax.dot_general(grad_gate, gate_w, LAST, preferred_element_type=F32)
        + lax.dot_general(grad_up, up_w, LAST, preferred_element_type=F32)
    ).astype(BF16)

    comb_part = jnp.sum(hidden.astype(F32) * grad_hidden, axis=1)
    inner_part = jnp.sum(grad_gate.astype(F32) * gate_pre + grad_up.astype(F32) * up_pre, axis=1)

    back_out = exchange(expert_out.reshape(region_count, capacity, D)).reshape(slot_total, D)
    out_sum = dot(weight_high, back_out) + dot(weight_low, back_out)
    moe_out = lax.psum_scatter(out_sum.astype(BF16), "local", scatter_dimension=1, tiled=True)

    scalars = exchange(jnp.stack([comb_part, inner_part], axis=1).reshape(region_count, capacity, 2))
    scalars = scalars.reshape(slot_total, 2)
    picked = jnp.sum(jnp.where(hits[:, :, :, None], scalars[None, None, :, :], 0.0), axis=2)
    picked = lax.psum(picked, "local")
    grad_combine = picked[:, :, 0]
    inner = jnp.sum(picked[:, :, 1] * combine, axis=1, keepdims=True) / inv_rms

    back_grad = exchange(branch_grad.reshape(region_count, capacity, D)).reshape(slot_total, D)
    grad_sum = dot(weight_high, back_grad) + dot(weight_low, back_grad)
    grad_normed = lax.psum_scatter(grad_sum.astype(BF16), "local", scatter_dimension=1, tiled=True)
    scaled = norm_gain * grad_normed.astype(F32)
    grad_tokens = (
        inv_rms * scaled - tokens.astype(F32) * inv_rms * inv_rms * inv_rms * inner / D
    ).astype(BF16)
    return (moe_out, grad_tokens, grad_combine)


def solution(mesh):
    placed = (
        P("region", "local"),
        P("local"),
        P("region", None, "local"),
        P("region", None, "local"),
        P("region", "local", None),
        P("region", None),
        P("region", None),
        P("region", "local"),
    )
    return jax.shard_map(
        on_device,
        mesh=mesh,
        in_specs=placed,
        out_specs=(P("region", "local"), P("region", "local"), P("region", None)),
        check_vma=False,
    )
```

time: 496 us -> 368 us (0.74)
  blocking collectives: 89.5 us -> 25 us
  waiting for transfers between devices: 273 us -> 225 us
  local copies, waits for them, and re-layouts: 45.3 us -> 4.13 us
  matrix products: 37.7 us -> 70.8 us
  other arithmetic: 22.7 us -> 5.79 us
  starting transfers between devices: 13.1 us -> 22.3 us
    reduce_scatter x2, waiting for transfers between devices: 155 us -> 15 us  [the longest x1 15 us: on_device(): lax.psum_scatter(out_sum.astype(BF16), 'local', scatter_dimension=1, tile...]
    all_to_all x3 -> x5, waiting for transfers between devices: 54.8 us -> 139 us  [exchange(): lax.all_to_all(blocks, 'region', split_axis=0, concat_axis=0, tiled=True)]
    all_to_all x1 -> x0, blocking collectives: 56.8 us -> none  [on_device(): lax.all_to_all(pack_rows(normed_full), 'region', split_axis=0, concat_axi...]
    gather x6 -> x0, local copies, waits for them, and re-layouts: 41.5 us -> none  [the longest x2 29.5 us: pack_rows(): picked = jnp.take(matrix, source, axis=0, mode='fill', fill_value=0)]
    dot_general x5 -> x13, matrix products: 37.7 us -> 70.8 us  [the longest x8 38.8 us: dot(): return jnp.dot(left, right, preferred_element_type=F32)]
    psum x2 -> x1, blocking collectives: 32.7 us -> 10.2 us  [on_device(): picked = lax.psum(picked, 'local')]
    all_gather x0 -> x1, blocking collectives: none -> 14.9 us  [on_device(): gain_full = lax.all_gather(norm_gain, 'local', axis=0, tiled=True)]
    all_to_all x3 -> x5, starting transfers between devices: 12.7 us -> 22.1 us  [exchange(): lax.all_to_all(blocks, 'region', split_axis=0, concat_axis=0, tiled=True)]
  transfers between devices with their start and end apart: 7 -> 9, of which waited for: 6 -> 8; matrix products, arithmetic and copies ran while one was open for 8% -> 14% of each run, Pallas kernels for 0% -> 0%
where the time goes in v1:
time: 368 us; the launch traced here: 367 us
  waiting for transfers between devices  225 us (61%)
  matrix products  70.8 us (19%)
  blocking collectives  25 us (7%)
  starting transfers between devices  22.3 us (6%)
  between operations  14 us (4%)
  other arithmetic  5.79 us (2%)
  local copies, waits for them, and re-layouts  4.13 us (1%)
    all_to_all x5, waiting for transfers between devices, exchange(): lax.all_to_all(blocks, 'region', split_axis=0, concat_axis=0, tiled=True)  139 us
    all_gather x1, waiting for transfers between devices, on_device(): grad_full = lax.all_gather(grad_out, 'local', axis=1, tiled=True)  42.4 us
    dot_general x8, matrix products, dot(): return jnp.dot(left, right, preferred_element_type=F32)  38.8 us
    all_gather x1, waiting for transfers between devices, on_device(): tokens_full = lax.all_gather(tokens, 'local', axis=1, tiled=True)  27.6 us
    all_to_all x5, starting transfers between devices, exchange(): lax.all_to_all(blocks, 'region', split_axis=0, concat_axis=0, tiled=True)  22.1 us
    reduce_scatter x1, waiting for transfers between devices, on_device(): lax.psum_scatter(out_sum.astype(BF16), 'local', scatter_dimension=1, tile...  15 us
    all_gather x1, blocking collectives, on_device(): gain_full = lax.all_gather(norm_gain, 'local', axis=0, tiled=True)  14.9 us
    psum x1, blocking collectives, on_device(): picked = lax.psum(picked, 'local')  10.2 us
  transfers between devices with their start and end apart: 9, of which 8 were waited for; matrix products, arithmetic and copies ran while one was open for 14% of the time, Pallas kernels for 0%

profile of v1, /device:TPU:0, one launch (start us, length us, event | category | flops | bytes accessed | tf_op | source)
XLA Modules:
  0.0 367.4 jit_solution(11772798937456941023)
XLA Ops:
  7.2 0.7 all-gather.4.cloned.1.call-update
  7.9 0.8 copy.36
  8.7 0.1 eq.32
  8.8 0.2 fusion.19
  9.0 0.1 convert_element_type.91
  9.2 0.1 copy.37
  9.2 0.7 reshape.75
  10.0 14.9 %all-gather = f32[4,1,1792]{2,1,0:T(1,128)S(1)} all-gather(f32[1,1,1792]{2,1,0:T(1,128)S(1)} %reshape.75), channel_id=1, replica_groups=mesh['region'=8,'local'=4] {'local'}, dimensions={0}, use_global_device_ids=true | all-gather | bytes 35840 | tf_op jit(solution)/shard_map/all_gather | solution.py:29
  24.8 0.7 multiply_add_fusion
  25.5 0.8 select_reduce_fusion.1
  26.3 27.6 %all-gather.4.cloned.1.call-done = bf16[128,7168]{1,0:T(8,128)(2,1)} async-done(((bf16[128,1792]{1,0:T(8,128)(2,1)}), bf16[128,7168]{1,0:T(8,128)(2,1)}) %all-gather.4.cloned.1.call-update) | async-done | bytes 1835024 | tf_op jit(solution)/shard_map/all_gather | solution.py:30
  53.9 1.9 fusion.13
  55.8 5.1 %convolution_convert_fusion.2 = bf16[320,7168]{1,0:T(8,128)(2,1)} fusion(bf16[128,7168]{1,0:T(8,128)(2,1)} %all-gather.4.cloned.1.call-done, f32[7168]{0:T(1024)S(1)} %bitcast.45, f32[128]{0:T(128)S(1)} %fusion.24, bf16[128,320]{0,1:T(8,128)(2,1)S(1)} %get-tuple-element.6), kind=kOutput, calls=%fused_computation.4 | convolution fusion | flops 593166336 | bytes 6533632 | tf_op jit(solution)/shard_map/dot_general | solution.py:46
  61.0 4.6 %all-to-all-start = ((bf16[8,40,7168]{2,1,0:T(8,128)(2,1)}), bf16[8,40,7168]{2,1,0:T(8,128)(2,1)}, u32[]{:S(2)}, u32[]{:S(2)}) async-start(bf16[8,40,7168]{2,1,0:T(8,128)(2,1)} %bitcast.43), calls=%async_computation | async-start | bytes 9175040 | tf_op jit(solution)/shard_map/all_to_all | solution.py:50
  65.6 0.7 all-gather.6.cloned.1.call-update
  66.3 42.4 %all-gather.6.cloned.1.call-done = bf16[128,7168]{1,0:T(8,128)(2,1)} async-done(((bf16[128,1792]{1,0:T(8,128)(2,1)}), bf16[128,7168]{1,0:T(8,128)(2,1)}) %all-gather.6.cloned.1.call-update) | async-done | bytes 1835024 | tf_op jit(solution)/shard_map/all_gather | solution.py:31
  108.7 5.0 %convolution_convert_fusion = bf16[320,7168]{1,0:T(8,128)(2,1)} fusion(bf16[128,7168]{1,0:T(8,128)(2,1)} %all-gather.6.cloned.1.call-done, bf16[128,320]{0,1:T(8,128)(2,1)S(1)} %get-tuple-element.6), kind=kOutput, calls=%fused_computation.2 | convolution fusion | flops 589496320 | bytes 6504448 | tf_op jit(solution)/shard_map/dot_general | solution.py:46
  113.7 5.2 %all-to-all-done = bf16[8,40,7168]{2,1,0:T(8,128)(2,1)} async-done(((bf16[8,40,7168]{2,1,0:T(8,128)(2,1)}), bf16[8,40,7168]{2,1,0:T(8,128)(2,1)}, u32[]{:S(2)}, u32[]{:S(2)}) %all-to-all-start) | async-done | bytes 4587552 | tf_op jit(solution)/shard_map/all_to_all | solution.py:50
  118.9 4.8 %all-to-all-start.2 = ((bf16[8,40,7168]{2,1,0:T(8,128)(2,1)}), bf16[8,40,7168]{2,1,0:T(8,128)(2,1)}, u32[]{:S(2)}, u32[]{:S(2)}) async-start(bf16[8,40,7168]{2,1,0:T(8,128)(2,1)} %bitcast.41), calls=%async_computation.3 | async-start | bytes 9175040 | tf_op jit(solution)/shard_map/all_to_all | solution.py:50
  123.7 7.0 %fusion.11 = f32[320,512]{1,0:T(8,128)S(1)} fusion(bf16[320,7168]{1,0:T(8,128)(2,1)} %bitcast.2, bf16[1,7168,512]{2,1,0:T(8,128)(2,1)} %param.10), kind=kOutput, calls=%fused_computation.17 | convolution fusion | flops 2348810240 | bytes 12582912 | tf_op jit(solution)/shard_map/dot_general | solution.py:13
  130.7 7.2 %fusion.7 = f32[320,512]{1,0:T(8,128)S(1)} fusion(bf16[320,7168]{1,0:T(8,128)(2,1)} %bitcast.2, bf16[1,7168,512]{2,1,0:T(8,128)(2,1)} %param.11), kind=kOutput, calls=%fused_computation.13 | convolution fusion | flops 2348810240 | bytes 12582912 | tf_op jit(solution)/shard_map/dot_general | solution.py:13
  137.9 38.9 %all-to-all-done.2 = bf16[8,40,7168]{2,1,0:T(8,128)(2,1)} async-done(((bf16[8,40,7168]{2,1,0:T(8,128)(2,1)}), bf16[8,40,7168]{2,1,0:T(8,128)(2,1)}, u32[]{:S(2)}, u32[]{:S(2)}) %all-to-all-start.2) | async-done | bytes 4587552 | tf_op jit(solution)/shard_map/all_to_all | solution.py:50
  176.8 7.5 %multiply_reduce_fusion = (f32[320]{0:T(512)S(1)}, f32[320]{0:T(512)S(1)}, bf16[320,512]{1,0:T(8,128)(2,1)S(1)}, f32[320,512]{1,0:T(8,128)S(1)}) fusion(f32[320,512]{1,0:T(8,128)S(1)} %fusion.7, f32[320,512]{1,0:T(8,128)S(1)} %fusion.11, bf16[320,7168]{1,0:T(8,128)(2,1)} %bitcast.9, bf16[1,512,7168]{2,1,0:T(8,128)(2,1)} %param.12), kind=kOutput, calls=%fused_computation.31 | convolution fusion | flops 2352741888 | bytes 14223872 | tf_op jit(solution)/shard_map/dot_general | solution.py:64
  184.3 0.8 copy-done.1
  185.2 6.2 %fusion.9 = f32[320,7168]{1,0:T(8,128)S(1)} fusion(bf16[1,7168,512]{2,1,0:T(8,128)(2,1)} %param.10, f32[320,512]{1,0:T(8,128)} %copy-done, f32[320,512]{1,0:T(8,128)S(1)} %get-tuple-element.10, f32[320,512]{1,0:T(8,128)} %copy-done.3), kind=kOutput, calls=%fused_computation.15 | convolution fusion | flops 2350448640 | bytes 18481152 | tf_op jit(solution)/shard_map/dot_general | solution.py:68
  191.3 8.3 %fusion = bf16[320,7168]{1,0:T(8,128)(2,1)} fusion(f32[320,7168]{1,0:T(8,128)S(1)} %fusion.9, bf16[1,7168,512]{2,1,0:T(8,128)(2,1)} %param.11, f32[320,512]{1,0:T(8,128)} %copy-done.1, f32[320,512]{1,0:T(8,128)} %copy-done), kind=kOutput, calls=%fused_computation.1 | convolution fusion | flops 2354380800 | bytes 22413312 | tf_op jit(solution)/shard_map/dot_general | solution.py:69
  199.6 4.8 %all-to-all-start.3 = ((bf16[8,40,7168]{2,1,0:T(8,128)(2,1)}), bf16[8,40,7168]{2,1,0:T(8,128)(2,1)}, u32[]{:S(2)}, u32[]{:S(2)}) async-start(bf16[8,40,7168]{2,1,0:T(8,128)(2,1)} %bitcast.42), calls=%async_computation.4 | async-start | bytes 9175040 | tf_op jit(solution)/shard_map/all_to_all | solution.py:50
  204.5 7.8 %convolution_convert_fusion.1 = bf16[320,7168]{1,0:T(8,128)(2,1)} fusion(bf16[320,512]{1,0:T(8,128)(2,1)S(1)} %get-tuple-element.7, bf16[1,512,7168]{2,1,0:T(8,128)(2,1)} %param.12), kind=kOutput, calls=%fused_computation.3 | convolution fusion | flops 2351104000 | bytes 12255232 | tf_op jit(solution)/shard_map/dot_general | solution.py:13
  212.2 45.3 %all-to-all-done.3 = bf16[8,40,7168]{2,1,0:T(8,128)(2,1)} async-done(((bf16[8,40,7168]{2,1,0:T(8,128)(2,1)}), bf16[8,40,7168]{2,1,0:T(8,128)(2,1)}, u32[]{:S(2)}, u32[]{:S(2)}) %all-to-all-start.3) | async-done | bytes 4587552 | tf_op jit(solution)/shard_map/all_to_all | solution.py:50
  257.6 4.6 %all-to-all-start.1 = ((bf16[8,40,7168]{2,1,0:T(8,128)(2,1)}), bf16[8,40,7168]{2,1,0:T(8,128)(2,1)}, u32[]{:S(2)}, u32[]{:S(2)}) async-start(bf16[8,40,7168]{2,1,0:T(8,128)(2,1)} %bitcast.44), calls=%async_computation.1 | async-start | bytes 9175040 | tf_op jit(solution)/shard_map/all_to_all | solution.py:50
  262.2 0.0 reduce-scatter.5.cloned.1.call-start
  262.2 3.5 fusion.25
  265.7 4.8 %fusion.2 = bf16[128,7168]{1,0:T(8,128)(2,1)} fusion(f32[128,7168]{1,0:T(8,128)S(1)} %fusion.25, bf16[320,7168]{1,0:T(8,128)(2,1)} %bitcast.11, f32[128,320]{0,1:T(8,128)S(1)} %get-tuple-element.5), kind=kOutput, calls=%fused_computation.8 | convolution fusion | flops 589201408 | bytes 10256384 | tf_op jit(solution)/shard_map/dot_general | solution.py:13
  270.5 45.0 %all-to-all-done.1 = bf16[8,40,7168]{2,1,0:T(8,128)(2,1)} async-done(((bf16[8,40,7168]{2,1,0:T(8,128)(2,1)}), bf16[8,40,7168]{2,1,0:T(8,128)(2,1)}, u32[]{:S(2)}, u32[]{:S(2)}) %all-to-all-start.1) | async-done | bytes 4587552 | tf_op jit(solution)/shard_map/all_to_all | solution.py:50
  315.5 3.5 fusion.27
  319.0 4.9 %fusion.1 = bf16[128,7168]{1,0:T(8,128)(2,1)} fusion(f32[128,7168]{1,0:T(8,128)S(1)} %fusion.27, bf16[320,7168]{1,0:T(8,128)(2,1)} %bitcast.7, f32[128,320]{0,1:T(8,128)S(1)} %get-tuple-element.5), kind=kOutput, calls=%fused_computation.7 | convolution fusion | flops 589201408 | bytes 10256384 | tf_op jit(solution)/shard_map/dot_general | solution.py:13
  323.9 0.1 stack.10
  324.0 0.1 stack.9
  324.1 0.6 copy.38
  324.7 3.3 all-to-all-start.4
  328.0 0.1 iota_compare_fusion
  328.1 4.6 %all-to-all-done.4 = f32[8,40,2]{1,2,0:T(2,128)S(1)} async-done(((f32[8,40,2]{1,2,0:T(2,128)}), f32[8,40,2]{1,2,0:T(2,128)S(1)}, u32[]{:S(2)}, u32[]{:S(2)}) %all-to-all-start.4) | async-done | bytes 2592 | tf_op jit(solution)/shard_map/all_to_all | solution.py:50
  332.7 0.1 broadcast_in_dim.47
  332.7 0.2 select_reduce_fusion
  332.9 10.2 %psum.7 = f32[128,2,2]{0,2,1:T(2,128)S(1)} all-reduce(f32[128,2,2]{0,2,1:T(2,128)S(1)} %select_reduce_fusion), channel_id=1, replica_groups=mesh['region'=8,'local'=4] {'local'}, use_global_device_ids=true, to_apply=%region_9.10 | all-reduce | flops 512 | bytes 4096 | tf_op jit(solution)/shard_map/psum | solution.py:82
  343.1 0.6 fusion.29
  343.7 2.1 subtract_convert_fusion
  345.9 15.0 %reduce-scatter.3.cloned.1.call-done = bf16[128,1792]{1,0:T(8,128)(2,1)} async-done(((bf16[128,7168]{1,0:T(8,128)(2,1)}), bf16[128,1792]{1,0:T(8,128)(2,1)}) %reduce-scatter.3.cloned.1.call-update) | async-done | bytes 458768 | tf_op jit(solution)/shard_map/reduce_scatter | solution.py:77
  (23 shorter events, 0.3 us)
Async XLA Ops:
  7.2 46.7 %all-gather.4.cloned.1.call-start = ((), (), s32[]{:S(2)}) async-start(), calls=%async_computation.7 | async-start | bytes 2293760 | tf_op jit(solution)/shard_map/all_gather | solution.py:30
  61.0 57.9 %all-to-all-start = ((bf16[8,40,7168]{2,1,0:T(8,128)(2,1)}), bf16[8,40,7168]{2,1,0:T(8,128)(2,1)}, u32[]{:S(2)}, u32[]{:S(2)}) async-start(bf16[8,40,7168]{2,1,0:T(8,128)(2,1)} %bitcast.43), calls=%async_computation | async-start | bytes 9175040 | tf_op jit(solution)/shard_map/all_to_all | solution.py:50
  65.6 43.2 %all-gather.6.cloned.1.call-start = ((), (), s32[]{:S(2)}) async-start(), calls=%async_computation.9 | async-start | bytes 2293760 | tf_op jit(solution)/shard_map/all_gather | solution.py:31
  118.9 57.9 %all-to-all-start.2 = ((bf16[8,40,7168]{2,1,0:T(8,128)(2,1)}), bf16[8,40,7168]{2,1,0:T(8,128)(2,1)}, u32[]{:S(2)}, u32[]{:S(2)}) async-start(bf16[8,40,7168]{2,1,0:T(8,128)(2,1)} %bitcast.41), calls=%async_computation.3 | async-start | bytes 9175040 | tf_op jit(solution)/shard_map/all_to_all | solution.py:50
  130.7 46.2 %copy-start = (f32[320,512]{1,0:T(8,128)}, f32[320,512]{1,0:T(8,128)S(1)}, u32[]{:S(2)}) copy-start(f32[320,512]{1,0:T(8,128)S(1)} %fusion.11) | copy-start | bytes 1966084
  137.9 46.4 %copy-start.3 = (f32[320,512]{1,0:T(8,128)}, f32[320,512]{1,0:T(8,128)S(1)}, u32[]{:S(2)}) copy-start(f32[320,512]{1,0:T(8,128)S(1)} %fusion.7) | copy-start | bytes 1966084
  184.3 0.9 copy-start.1
  199.6 57.9 %all-to-all-start.3 = ((bf16[8,40,7168]{2,1,0:T(8,128)(2,1)}), bf16[8,40,7168]{2,1,0:T(8,128)(2,1)}, u32[]{:S(2)}, u32[]{:S(2)}) async-start(bf16[8,40,7168]{2,1,0:T(8,128)(2,1)} %bitcast.42), calls=%async_computation.4 | async-start | bytes 9175040 | tf_op jit(solution)/shard_map/all_to_all | solution.py:50
  257.6 57.9 %all-to-all-start.1 = ((bf16[8,40,7168]{2,1,0:T(8,128)(2,1)}), bf16[8,40,7168]{2,1,0:T(8,128)(2,1)}, u32[]{:S(2)}, u32[]{:S(2)}) async-start(bf16[8,40,7168]{2,1,0:T(8,128)(2,1)} %bitcast.44), calls=%async_computation.1 | async-start | bytes 9175040 | tf_op jit(solution)/shard_map/all_to_all | solution.py:50
  262.2 81.5 %reduce-scatter.5.cloned.1.call-start = ((), (), s32[]{:S(2)}) async-start(), calls=%async_computation.10 | async-start | bytes 2293760 | tf_op jit(solution)/shard_map/reduce_scatter | solution.py:88
  270.5 90.3 %reduce-scatter.3.cloned.1.call-start = ((), (), s32[]{:S(2)}) async-start(), calls=%async_computation.8 | async-start | bytes 2293760 | tf_op jit(solution)/shard_map/reduce_scatter | solution.py:77
  319.0 24.7 %copy-start.5 = (f32[128,2]{0,1:T(2,128)S(1)}, f32[128,2]{0,1:T(2,128)}, u32[]{:S(2)}) copy-start(f32[128,2]{0,1:T(2,128)} %param.14) | copy-start | bytes 3076
  319.0 24.7 %copy-start.2 = (bf16[128,1792]{1,0:T(8,128)(2,1)S(1)}, bf16[128,1792]{1,0:T(8,128)(2,1)}, u32[]{:S(2)}) copy-start(bf16[128,1792]{1,0:T(8,128)(2,1)} %param.8) | copy-start | bytes 1376260
  319.0 24.7 %copy-start.4 = (f32[1792]{0:T(1024)S(1)}, f32[1792]{0:T(1024)}, u32[]{:S(2)}) copy-start(f32[1792]{0:T(1024)} %param.9) | copy-start | bytes 21508
  324.7 8.0 %all-to-all-start.4 = ((f32[8,40,2]{1,2,0:T(2,128)}), f32[8,40,2]{1,2,0:T(2,128)S(1)}, u32[]{:S(2)}, u32[]{:S(2)}) async-start(f32[8,40,2]{1,2,0:T(2,128)} %copy.38), calls=%async_computation.6 | async-start | bytes 16384 | tf_op jit(solution)/shard_map/all_to_all | solution.py:50
Sparse Core Ops, SparseCore 0:
  9.6 44.2 all-gather.3
  68.0 40.7 all-gather.5
  270.6 38.7 reduce-scatter.4
  324.0 36.7 reduce-scatter.2

commit v2 on v1

--- a/solution.py
+++ b/solution.py
@@ -26,9 +26,21 @@
     slot_total = region_count * capacity
     gate_w, up_w, down_w = w_gate[0], w_up[0], w_down[0]
 
-    gain_full = lax.all_gather(norm_gain, "local", axis=0, tiled=True)
-    tokens_full = lax.all_gather(tokens, "local", axis=1, tiled=True)
-    grad_full = lax.all_gather(grad_out, "local", axis=1, tiled=True)
+    near = width_local // 256 * 128
+    far = width_local - near
+    share_count = lax.axis_size("local")
+
+    def gather(matrix):
+        return lax.all_gather(matrix, "local", axis=1, tiled=True)
+
+    def scatter(matrix):
+        width = matrix.shape[1] // share_count
+        stacked = jnp.stack([matrix[:, z * width:(z + 1) * width] for z in range(share_count)])
+        return lax.psum_scatter(stacked, "local", scatter_dimension=0, tiled=False)
+
+    def columns(matrix, start, width):
+        cuts = [lax.slice_in_dim(matrix, z * width_local + start, z * width_local + start + width, axis=1) for z in range(share_count)]
+        return jnp.concatenate(cuts, axis=1)
 
     flat_routes = regions.reshape(-1)
     one_hot = (flat_routes[:, None] == jnp.arange(region_count, dtype=jnp.int32)[None, :]).astype(F32)
@@ -49,11 +61,28 @@
     def exchange(blocks):
         return lax.all_to_all(blocks, "region", split_axis=0, concat_axis=0, tiled=True)
 
-    inputs_full = tokens_full.astype(F32)
+    grad_near = gather(grad_out[:, :near])
+    far_blocks = exchange(pack_rows(grad_out[:, near:])).reshape(slot_total, far)
+    gain_high, gain_rest = split_weights(norm_gain)
+    gain_mid, gain_low = split_weights(norm_gain - gain_high.astype(F32))
+    gain_rows = jnp.stack([gain_high, gain_mid, gain_low])
+    tokens_cat = jnp.concatenate([tokens, jnp.pad(gain_rows, ((0, 5), (0, 0)))], axis=0)
+    tokens_cat, grad_near = lax.optimization_barrier((tokens_cat, grad_near))
+    tokens_full = gather(tokens_cat)
+    near_rows = exchange(pack_rows(grad_near)).reshape(slot_total, share_count * near)
+    far_blocks, tokens_full = lax.optimization_barrier((far_blocks, tokens_full))
+    far_rows = gather(far_blocks)
+
+    gain_full = jnp.sum(tokens_full[token_count:token_count + 3].astype(F32), axis=0)
+    inputs_full = tokens_full[:token_count].astype(F32)
     inv_rms = lax.rsqrt(jnp.sum(inputs_full * inputs_full, axis=1, keepdims=True) / D + 1e-06)
     normed = (inputs_full * inv_rms * gain_full).astype(BF16)
     rows_in = exchange(pack_rows(normed)).reshape(slot_total, D)
-    rows_grad = exchange(pack_rows(grad_full)).reshape(slot_total, D)
+    pieces = []
+    for z in range(share_count):
+        pieces.append(near_rows[:, z * near:(z + 1) * near])
+        pieces.append(far_rows[:, z * far:(z + 1) * far])
+    rows_grad = jnp.concatenate(pieces, axis=1)
 
     gate_pre = dot(rows_in, gate_w)
     up_pre = dot(rows_in, up_w)
@@ -72,20 +101,40 @@
     comb_part = jnp.sum(hidden.astype(F32) * grad_hidden, axis=1)
     inner_part = jnp.sum(grad_gate.astype(F32) * gate_pre + grad_up.astype(F32) * up_pre, axis=1)
 
-    back_out = exchange(expert_out.reshape(region_count, capacity, D)).reshape(slot_total, D)
-    out_sum = dot(weight_high, back_out) + dot(weight_low, back_out)
-    moe_out = lax.psum_scatter(out_sum.astype(BF16), "local", scatter_dimension=1, tiled=True)
+    scalars = jnp.stack([comb_part, inner_part], axis=1)
+    scalars = jnp.concatenate(split_weights(scalars), axis=1)
+    scalars = jnp.pad(scalars, ((0, 0), (0, 124)))
 
-    scalars = exchange(jnp.stack([comb_part, inner_part], axis=1).reshape(region_count, capacity, 2))
-    scalars = scalars.reshape(slot_total, 2)
-    picked = jnp.sum(jnp.where(hits[:, :, :, None], scalars[None, None, :, :], 0.0), axis=2)
-    picked = lax.psum(picked, "local")
+    def send_home(rows):
+        return exchange(rows.reshape(region_count, capacity, rows.shape[1])).reshape(slot_total, rows.shape[1])
+
+    def combined(rows):
+        return dot(weight_high, rows) + dot(weight_low, rows)
+
+    out_far = scatter(columns(expert_out, near, far))
+    near_sent = jnp.concatenate([columns(expert_out, 0, near), scalars], axis=1)
+    out_near = send_home(near_sent)
+    early = send_home(columns(branch_grad, 0, near))
+    out_near, out_far = lax.optimization_barrier((out_near, out_far))
+    scalars = out_near[:, share_count * near:]
+    picked = jnp.einsum("tks,sc->tkc", hits.astype(BF16), scalars, preferred_element_type=F32)
+    picked = lax.psum(picked[:, :, :2] + picked[:, :, 2:4], "local")
     grad_combine = picked[:, :, 0]
     inner = jnp.sum(picked[:, :, 1] * combine, axis=1, keepdims=True) / inv_rms
 
-    back_grad = exchange(branch_grad.reshape(region_count, capacity, D)).reshape(slot_total, D)
-    grad_sum = dot(weight_high, back_grad) + dot(weight_low, back_grad)
-    grad_normed = lax.psum_scatter(grad_sum.astype(BF16), "local", scatter_dimension=1, tiled=True)
+    moe_near = scatter(combined(out_near[:, :share_count * near]).astype(BF16))
+    out_far, early = lax.optimization_barrier((out_far, early))
+    back_far = send_home(out_far)
+    moe_far = combined(back_far).astype(BF16)
+    moe_out = jnp.concatenate([moe_near, moe_far], axis=1)
+
+    early = combined(early).astype(BF16)
+    late, back_far, early = lax.optimization_barrier((columns(branch_grad, near, far), back_far, early))
+    early = scatter(early)
+    late = send_home(late)
+    late, inner = lax.optimization_barrier((late, inner))
+    late = scatter(combined(late).astype(BF16))
+    grad_normed = jnp.concatenate([early, late], axis=1)
     scaled = norm_gain * grad_normed.astype(F32)
     grad_tokens = (
         inv_rms * scaled - tokens.astype(F32) * inv_rms * inv_rms * inv_rms * inner / D

time: 368 us -> 317 us (0.86)
  waiting for transfers between devices: 225 us -> 146 us
  matrix products: 70.8 us -> 52.1 us
  local copies, waits for them, and re-layouts: 4.13 us -> 20.6 us
  other arithmetic: 5.79 us -> 22.2 us
  blocking collectives: 25 us -> 32.5 us
  starting transfers between devices: 22.3 us -> 27.9 us
    all_to_all x5 -> x7, waiting for transfers between devices: 139 us -> 64.7 us  [exchange(): lax.all_to_all(blocks, 'region', split_axis=0, concat_axis=0, tiled=True)]
    dot_general x8 -> x12, matrix products: 38.8 us -> 24 us  [dot(): return jnp.dot(left, right, preferred_element_type=F32)]
    all_gather x2, waiting for transfers between devices: 70 us -> 58.8 us  [gather(): return lax.all_gather(matrix, 'local', axis=1, tiled=True)]
    unnamed x14 -> x45, local copies, waits for them, and re-layouts: 2.39 us -> 10.6 us
    concatenate x0 -> x5, other arithmetic: none -> 8.07 us  [the longest x2 4.47 us: columns(): return jnp.concatenate(cuts, axis=1)]
    all_gather x1, blocking collectives: 14.9 us -> 22.8 us  [gather(): return lax.all_gather(matrix, 'local', axis=1, tiled=True)]
    reduce_scatter x2 -> x4, waiting for transfers between devices: 15 us -> 22.7 us  [scatter(): return lax.psum_scatter(stacked, 'local', scatter_dimension=0, tiled=False)]
    all_to_all x5 -> x7, starting transfers between devices: 22.1 us -> 27.5 us  [exchange(): lax.all_to_all(blocks, 'region', split_axis=0, concat_axis=0, tiled=True)]
  transfers between devices with their start and end apart: 9 -> 13, of which waited for: 8 -> 10; matrix products, arithmetic and copies ran while one was open for 14% -> 20% of each run, Pallas kernels for 0% -> 0%
where the time goes in v2:
time: 317 us; the launch traced here: 316 us
  waiting for transfers between devices  146 us (46%)
  matrix products  52.1 us (16%)
  blocking collectives  32.5 us (10%)
  starting transfers between devices  27.9 us (9%)
  other arithmetic  22.2 us (7%)
  local copies, waits for them, and re-layouts  20.6 us (6%)
  between operations  14.5 us (5%)
    all_to_all x7, waiting for transfers between devices, exchange(): lax.all_to_all(blocks, 'region', split_axis=0, concat_axis=0, tiled=True)  64.7 us
    all_gather x2, waiting for transfers between devices, gather(): return lax.all_gather(matrix, 'local', axis=1, tiled=True)  58.8 us
    all_to_all x7, starting transfers between devices, exchange(): lax.all_to_all(blocks, 'region', split_axis=0, concat_axis=0, tiled=True)  27.5 us
    dot_general x12, matrix products, dot(): return jnp.dot(left, right, preferred_element_type=F32)  24 us
    all_gather x1, blocking collectives, gather(): return lax.all_gather(matrix, 'local', axis=1, tiled=True)  22.8 us
    reduce_scatter x4, waiting for transfers between devices, scatter(): return lax.psum_scatter(stacked, 'local', scatter_dimension=0, tiled=False)  22.7 us
    unnamed x45, local copies, waits for them, and re-layouts  10.6 us
    psum x1, blocking collectives, on_device(): picked = lax.psum(picked[:, :, :2] + picked[:, :, 2:4], 'local')  9.71 us
  transfers between devices with their start and end apart: 13, of which 10 were waited for; matrix products, arithmetic and copies ran while one was open for 20% of the time, Pallas kernels for 0%

profile of v2, /device:TPU:0, one launch (start us, length us, event | category | flops | bytes accessed | tf_op | source)
XLA Modules:
  0.0 316.2 jit_solution(8868454749101293518)
XLA Ops:
  9.0 22.8 %all_gather.9 = bf16[128,3584]{1,0:T(8,128)(2,1)S(1)} all-gather(bf16[128,896]{1,0:T(8,128)(2,1)S(1)} %slice.139), channel_id=1, replica_groups=mesh['region'=8,'local'=4] {'local'}, dimensions={1}, use_global_device_ids=true | all-gather | bytes 1146880 | tf_op jit(solution)/shard_map/all_gather | solution.py:34
  31.9 1.9 pad_maximum_fusion.6
  35.2 1.1 convolution_convert_fusion.3
  36.3 3.7 %all-to-all-start = ((bf16[8,40,896]{2,1,0:T(8,128)(2,1)}), bf16[8,40,896]{2,1,0:T(8,128)(2,1)S(1)}, u32[]{:S(2)}, u32[]{:S(2)}) async-start(bf16[8,40,896]{2,1,0:T(8,128)(2,1)} %bitcast), calls=%async_computation | async-start | bytes 1146880 | tf_op jit(solution)/shard_map/all_to_all | solution.py:62
  40.0 2.2 convolution_convert_fusion.2
  42.2 8.1 %all-to-all-done = bf16[8,40,896]{2,1,0:T(8,128)(2,1)S(1)} async-done(((bf16[8,40,896]{2,1,0:T(8,128)(2,1)}), bf16[8,40,896]{2,1,0:T(8,128)(2,1)S(1)}, u32[]{:S(2)}, u32[]{:S(2)}) %all-to-all-start) | async-done | bytes 573472 | tf_op jit(solution)/shard_map/all_to_all | solution.py:62
  50.3 3.6 %all-to-all-start.2 = ((bf16[8,40,3584]{2,1,0:T(8,128)(2,1)}), bf16[8,40,3584]{2,1,0:T(8,128)(2,1)S(1)}, u32[]{:S(2)}, u32[]{:S(2)}) async-start(bf16[8,40,3584]{2,1,0:T(8,128)(2,1)} %bitcast.7), calls=%async_computation.2 | async-start | bytes 4587520 | tf_op jit(solution)/shard_map/all_to_all | solution.py:62
  54.0 22.7 %all-gather.3.cloned.1.call-done = bf16[136,7168]{1,0:T(8,128)(2,1)} async-done(((bf16[136,1792]{1,0:T(8,128)(2,1)}), bf16[136,7168]{1,0:T(8,128)(2,1)}) %all-gather.3.cloned.1.call-update) | async-done | bytes 1949712 | tf_op jit(solution)/shard_map/all_gather | solution.py:34
  76.7 1.0 convert_reduce_fusion.1
  77.7 1.9 fusion.14
  79.6 5.0 %convolution_convert_fusion.1 = bf16[320,7168]{1,0:T(8,128)(2,1)} fusion(f32[7168]{0:T(1024)S(1)} %convert_reduce_fusion.1, f32[128]{0:T(128)S(1)} %fusion.40, bf16[136,7168]{1,0:T(8,128)(2,1)} %all-gather.3.cloned.1.call-done, bf16[128,320]{0,1:T(8,128)(2,1)S(1)} %get-tuple-element.29), kind=kOutput, calls=%fused_computation.3 | convolution fusion | flops 593166336 | bytes 6533632 | tf_op jit(solution)/shard_map/dot_general | solution.py:58
  84.7 4.6 %all-to-all-start.1 = ((bf16[8,40,7168]{2,1,0:T(8,128)(2,1)}), bf16[8,40,7168]{2,1,0:T(8,128)(2,1)}, u32[]{:S(2)}, u32[]{:S(2)}) async-start(bf16[8,40,7168]{2,1,0:T(8,128)(2,1)} %bitcast.97), calls=%async_computation.1 | async-start | bytes 9175040 | tf_op jit(solution)/shard_map/all_to_all | solution.py:62
  90.4 36.1 %all-gather.5.cloned.1.call-done = bf16[320,3584]{1,0:T(8,128)(2,1)} async-done(((bf16[320,896]{1,0:T(8,128)(2,1)}), bf16[320,3584]{1,0:T(8,128)(2,1)}) %all-gather.5.cloned.1.call-update) | async-done | bytes 2293776 | tf_op jit(solution)/shard_map/all_gather | solution.py:34
  126.5 2.1 slice_dynamic-update-slice_fusion.6
  134.2 8.4 %all-to-all-done.1 = bf16[8,40,7168]{2,1,0:T(8,128)(2,1)} async-done(((bf16[8,40,7168]{2,1,0:T(8,128)(2,1)}), bf16[8,40,7168]{2,1,0:T(8,128)(2,1)}, u32[]{:S(2)}, u32[]{:S(2)}) %all-to-all-start.1) | async-done | bytes 4587552 | tf_op jit(solution)/shard_map/all_to_all | solution.py:62
  142.6 7.1 %fusion.9 = f32[320,512]{1,0:T(8,128)S(1)} fusion(bf16[320,7168]{1,0:T(8,128)(2,1)} %bitcast.3, bf16[1,7168,512]{2,1,0:T(8,128)(2,1)} %param.10), kind=kOutput, calls=%fused_computation.12 | convolution fusion | flops 2348810240 | bytes 12582912 | tf_op jit(solution)/shard_map/dot_general | solution.py:13
  149.8 5.1 %fusion.5 = f32[320,512]{1,0:T(8,128)S(1)} fusion(bf16[320,7168]{1,0:T(8,128)(2,1)} %bitcast.3, bf16[1,7168,512]{2,1,0:T(8,128)(2,1)S(1)} %bitcast.109), kind=kOutput, calls=%fused_computation.8 | convolution fusion | flops 2348810240 | bytes 12582912 | tf_op jit(solution)/shard_map/dot_general | solution.py:13
  155.0 3.7 %multiply_reduce_fusion = (f32[320]{0:T(512)S(1)}, f32[320]{0:T(512)S(1)}, bf16[320,512]{1,0:T(8,128)(2,1)S(1)}, f32[320,512]{1,0:T(8,128)}) fusion(f32[320,512]{1,0:T(8,128)S(1)} %fusion.5, f32[320,512]{1,0:T(8,128)S(1)} %fusion.9, bf16[320,7168]{1,0:T(8,128)(2,1)S(1)} %bitcast.118, bf16[1,512,7168]{2,1,0:T(8,128)(2,1)S(1)} %bitcast.123), kind=kOutput, calls=%fused_computation.47 | convolution fusion | flops 2352741888 | bytes 14223872 | tf_op jit(solution)/shard_map/dot_general | solution.py:93
  158.7 2.7 convolution_convert_fusion
  164.1 1.2 slice_bitcast_fusion.3
  165.3 1.7 pad_maximum_fusion
  168.0 4.8 %all-to-all-start.3 = ((bf16[8,40,3712]{2,1,0:T(8,128)(2,1)}), bf16[8,40,3712]{2,1,0:T(8,128)(2,1)}, u32[]{:S(2)}, u32[]{:S(2)}) async-start(bf16[8,40,3712]{2,1,0:T(8,128)(2,1)} %bitcast.9), calls=%async_computation.3 | async-start | bytes 4751360 | tf_op jit(solution)/shard_map/all_to_all | solution.py:62
  172.8 6.2 %fusion.7 = f32[320,7168]{1,0:T(8,128)S(1)} fusion(bf16[1,7168,512]{2,1,0:T(8,128)(2,1)} %param.10, f32[320,512]{1,0:T(8,128)S(1)} %copy-done.1, f32[320,512]{1,0:T(8,128)} %get-tuple-element.64, f32[320,512]{1,0:T(8,128)} %copy-done.6), kind=kOutput, calls=%fused_computation.10 | convolution fusion | flops 2350448640 | bytes 18481152 | tf_op jit(solution)/shard_map/dot_general | solution.py:97
  179.0 8.2 %fusion = bf16[320,7168]{1,0:T(8,128)(2,1)} fusion(f32[320,7168]{1,0:T(8,128)S(1)} %fusion.7, bf16[1,7168,512]{2,1,0:T(8,128)(2,1)} %param.11, f32[320,512]{1,0:T(8,128)} %get-tuple-element.64, f32[320,512]{1,0:T(8,128)S(1)} %copy-done.1), kind=kOutput, calls=%fused_computation.1 | convolution fusion | flops 2354380800 | bytes 22413312 | tf_op jit(solution)/shard_map/dot_general | solution.py:98
  187.2 3.7 %fusion.44 = (bf16[320,896]{1,0:T(8,128)(2,1)S(1)}, bf16[320,896]{1,0:T(8,128)(2,1)S(1)}, bf16[320,896]{1,0:T(8,128)(2,1)}, bf16[320,896]{1,0:T(8,128)(2,1)}, bf...) fusion(bf16[320,7168]{1,0:T(8,128)(2,1)} %fusion), kind=kLoop, calls=%fused_computation.119 | loop fusion | bytes 9175040 | tf_op jit(solution)/shard_map/slice | solution.py:42
  190.9 1.6 pad_maximum_fusion.1
  192.4 9.7 %all-to-all-done.3 = bf16[8,40,3712]{2,1,0:T(8,128)(2,1)} async-done(((bf16[8,40,3712]{2,1,0:T(8,128)(2,1)}), bf16[8,40,3712]{2,1,0:T(8,128)(2,1)}, u32[]{:S(2)}, u32[]{:S(2)}) %all-to-all-start.3) | async-done | bytes 2375712 | tf_op jit(solution)/shard_map/all_to_all | solution.py:62
  202.2 3.6 %all-to-all-start.4 = ((bf16[8,40,3584]{2,1,0:T(8,128)(2,1)}), bf16[8,40,3584]{2,1,0:T(8,128)(2,1)S(1)}, u32[]{:S(2)}, u32[]{:S(2)}) async-start(bf16[8,40,3584]{2,1,0:T(8,128)(2,1)} %bitcast.107), calls=%async_computation.6 | async-start | bytes 4587520 | tf_op jit(solution)/shard_map/all_to_all | solution.py:62
  205.9 1.7 subtract_convert_fusion.1
  207.5 2.9 pad_maximum_fusion.2
  210.4 1.1 reduce-scatter.5.cloned.1.call-done
  211.5 2.3 fusion.18
  213.8 2.3 fusion.11
  216.2 1.1 pad_maximum_fusion.3
  217.3 17.2 %all-to-all-done.4 = bf16[8,40,3584]{2,1,0:T(8,128)(2,1)S(1)} async-done(((bf16[8,40,3584]{2,1,0:T(8,128)(2,1)}), bf16[8,40,3584]{2,1,0:T(8,128)(2,1)S(1)}, u32[]{:S(2)}, u32[]{:S(2)}) %all-to-all-start.4) | async-done | bytes 2293792 | tf_op jit(solution)/shard_map/all_to_all | solution.py:62
  234.5 3.5 %all-to-all-start.5 = ((bf16[8,40,896]{2,1,0:T(8,128)(2,1)}), bf16[8,40,896]{2,1,0:T(8,128)(2,1)S(1)}, u32[]{:S(2)}, u32[]{:S(2)}) async-start(bf16[8,40,896]{2,1,0:T(8,128)(2,1)} %bitcast.113), calls=%async_computation.7 | async-start | bytes 1146880 | tf_op jit(solution)/shard_map/all_to_all | solution.py:62
  238.7 1.6 fusion.12
  240.3 7.9 %all-to-all-done.5 = bf16[8,40,896]{2,1,0:T(8,128)(2,1)S(1)} async-done(((bf16[8,40,896]{2,1,0:T(8,128)(2,1)}), bf16[8,40,896]{2,1,0:T(8,128)(2,1)S(1)}, u32[]{:S(2)}, u32[]{:S(2)}) %all-to-all-start.5) | async-done | bytes 573472 | tf_op jit(solution)/shard_map/all_to_all | solution.py:62
  248.2 3.6 %all-to-all-start.6 = ((bf16[8,40,3584]{2,1,0:T(8,128)(2,1)}), bf16[8,40,3584]{2,1,0:T(8,128)(2,1)S(1)}, u32[]{:S(2)}, u32[]{:S(2)}) async-start(bf16[8,40,3584]{2,1,0:T(8,128)(2,1)} %bitcast.106), calls=%async_computation.9 | async-start | bytes 4587520 | tf_op jit(solution)/shard_map/all_to_all | solution.py:62
  251.9 1.8 fusion.27
  253.7 1.4 slice_bitcast_fusion.15
  255.1 1.1 pad_maximum_fusion.4
  257.0 9.7 %psum.7 = f32[128,2,2]{0,2,1:T(2,128)S(1)} all-reduce(f32[128,2,2]{0,2,1:T(2,128)S(1)} %slice_add_fusion), channel_id=1, replica_groups=mesh['region'=8,'local'=4] {'local'}, use_global_device_ids=true, to_apply=%region_10.11 | all-reduce | flops 512 | bytes 4096 | tf_op jit(solution)/shard_map/psum | solution.py:121
  267.3 13.2 %all-to-all-done.6 = bf16[8,40,3584]{2,1,0:T(8,128)(2,1)S(1)} async-done(((bf16[8,40,3584]{2,1,0:T(8,128)(2,1)}), bf16[8,40,3584]{2,1,0:T(8,128)(2,1)S(1)}, u32[]{:S(2)}, u32[]{:S(2)}) %all-to-all-start.6) | async-done | bytes 2293792 | tf_op jit(solution)/shard_map/all_to_all | solution.py:62
  282.0 1.1 pad_maximum_fusion.5
  283.8 1.7 pad_maximum_fusion.7
  285.5 21.6 %reduce-scatter.11.cloned.1.call-done = bf16[1,128,896]{2,1,0:T(8,128)(2,1)} async-done(((bf16[4,128,896]{2,1,0:T(8,128)(2,1)}), bf16[1,128,896]{2,1,0:T(8,128)(2,1)}) %reduce-scatter.11.cloned.1.call-update) | async-done | bytes 229392 | tf_op jit(solution)/shard_map/reduce_scatter | solution.py:39
  307.2 2.2 subtract_convert_fusion
  (95 shorter events, 18.0 us)
Async XLA Ops:
  7.2 28.0 %copy-start.7 = (bf16[128,1792]{1,0:T(8,128)(2,1)S(1)}, bf16[128,1792]{1,0:T(8,128)(2,1)}, u32[]{:S(2)}) copy-start(bf16[128,1792]{1,0:T(8,128)(2,1)} %param.15) | copy-start | bytes 1376260
  7.2 26.6 %copy-start.9 = (s32[128,2]{0,1:T(2,128)S(1)}, s32[128,2]{0,1:T(2,128)}, u32[]{:S(2)}) copy-start(s32[128,2]{0,1:T(2,128)} %param.13) | copy-start | bytes 3076
  7.2 27.2 %copy-start.10 = (f32[128,2]{0,1:T(2,128)S(1)}, f32[128,2]{0,1:T(2,128)}, u32[]{:S(2)}) copy-start(f32[128,2]{0,1:T(2,128)} %param.14) | copy-start | bytes 3076
  7.2 69.5 %all-gather.3.cloned.1.call-start = ((), (), s32[]{:S(2)}) async-start(), calls=%async_computation.11 | async-start | bytes 2437120 | tf_op jit(solution)/shard_map/all_gather | solution.py:34
  36.3 14.0 %all-to-all-start = ((bf16[8,40,896]{2,1,0:T(8,128)(2,1)}), bf16[8,40,896]{2,1,0:T(8,128)(2,1)S(1)}, u32[]{:S(2)}, u32[]{:S(2)}) async-start(bf16[8,40,896]{2,1,0:T(8,128)(2,1)} %bitcast), calls=%async_computation | async-start | bytes 1146880 | tf_op jit(solution)/shard_map/all_to_all | solution.py:62
  50.3 26.4 %copy-start.3 = (bf16[8,40,896]{2,1,0:T(8,128)(2,1)}, bf16[8,40,896]{2,1,0:T(8,128)(2,1)S(1)}, u32[]{:S(2)}) copy-start(bf16[8,40,896]{2,1,0:T(8,128)(2,1)S(1)} %all-to-all-done) | copy-start | bytes 1720324
  50.3 34.4 %all-to-all-start.2 = ((bf16[8,40,3584]{2,1,0:T(8,128)(2,1)}), bf16[8,40,3584]{2,1,0:T(8,128)(2,1)S(1)}, u32[]{:S(2)}, u32[]{:S(2)}) async-start(bf16[8,40,3584]{2,1,0:T(8,128)(2,1)} %bitcast.7), calls=%async_computation.2 | async-start | bytes 4587520 | tf_op jit(solution)/shard_map/all_to_all | solution.py:62
  53.9 72.6 %all-gather.5.cloned.1.call-start = ((), (), s32[]{:S(2)}) async-start(), calls=%async_computation.12 | async-start | bytes 2867200 | tf_op jit(solution)/shard_map/all_gather | solution.py:34
  84.7 57.9 %all-to-all-start.1 = ((bf16[8,40,7168]{2,1,0:T(8,128)(2,1)}), bf16[8,40,7168]{2,1,0:T(8,128)(2,1)}, u32[]{:S(2)}, u32[]{:S(2)}) async-start(bf16[8,40,7168]{2,1,0:T(8,128)(2,1)} %bitcast.97), calls=%async_computation.1 | async-start | bytes 9175040 | tf_op jit(solution)/shard_map/all_to_all | solution.py:62
  89.3 122.2 %reduce-scatter.5.cloned.1.call-start = ((), (), s32[]{:S(2)}) async-start(), calls=%async_computation.13 | async-start | bytes 2867200 | tf_op jit(solution)/shard_map/reduce_scatter | solution.py:39
  126.5 3.0 copy-start.2
  133.3 16.5 %slice-start = ((s8[7340032]{0:T(1024)(128)(4,1)}), s8[3145728]{0:T(1024)(128)(4,1)S(1)}, s32[]{:S(2)}) async-start(s8[7340032]{0:T(1024)(128)(4,1)} %bitcast.108), calls=%async_computation.17 | async-start | bytes 6291456
  142.6 7.2 %slice-start.1 = ((s8[7340032]{0:T(1024)(128)(4,1)}), s8[4194304]{0:T(1024)(128)(4,1)S(1)}, s32[]{:S(2)}) async-start(s8[7340032]{0:T(1024)(128)(4,1)} %bitcast.108), calls=%async_computation.18 | async-start | bytes 8388608
  142.6 12.3 %slice-start.2 = ((s8[4587520]{0:T(1024)(128)(4,1)}), s8[4194304]{0:T(1024)(128)(4,1)S(1)}, s32[]{:S(2)}) async-start(s8[4587520]{0:T(1024)(128)(4,1)} %bitcast.117), calls=%async_computation.19 | async-start | bytes 8388608
  142.6 12.3 %slice-start.4 = ((s8[7340032]{0:T(1024)(128)(4,1)}), s8[4194304]{0:T(1024)(128)(4,1)S(1)}, s32[]{:S(2)}) async-start(s8[7340032]{0:T(1024)(128)(4,1)} %bitcast.122), calls=%async_computation.21 | async-start | bytes 8388608
  149.8 5.1 %copy-start = (f32[320,512]{1,0:T(8,128)}, f32[320,512]{1,0:T(8,128)S(1)}, u32[]{:S(2)}) copy-start(f32[320,512]{1,0:T(8,128)S(1)} %fusion.9) | copy-start | bytes 1966084
  149.8 5.1 %slice-start.3 = ((s8[4587520]{0:T(1024)(128)(4,1)}), s8[393216]{0:T(1024)(128)(4,1)S(1)}, s32[]{:S(2)}) async-start(s8[4587520]{0:T(1024)(128)(4,1)} %bitcast.117), calls=%async_computation.20 | async-start | bytes 786432
  149.8 5.1 %slice-start.5 = ((s8[7340032]{0:T(1024)(128)(4,1)}), s8[3145728]{0:T(1024)(128)(4,1)S(1)}, s32[]{:S(2)}) async-start(s8[7340032]{0:T(1024)(128)(4,1)} %bitcast.122), calls=%async_computation.22 | async-start | bytes 6291456
  155.0 3.7 %copy-start.6 = (f32[320,512]{1,0:T(8,128)}, f32[320,512]{1,0:T(8,128)S(1)}, u32[]{:S(2)}) copy-start(f32[320,512]{1,0:T(8,128)S(1)} %fusion.5) | copy-start | bytes 1966084
  168.0 4.8 %copy-start.1 = (f32[320,512]{1,0:T(8,128)S(1)}, f32[320,512]{1,0:T(8,128)}, u32[]{:S(2)}) copy-start(f32[320,512]{1,0:T(8,128)} %copy-done) | copy-start | bytes 1966084
  168.0 34.2 %all-to-all-start.3 = ((bf16[8,40,3712]{2,1,0:T(8,128)(2,1)}), bf16[8,40,3712]{2,1,0:T(8,128)(2,1)}, u32[]{:S(2)}, u32[]{:S(2)}) async-start(bf16[8,40,3712]{2,1,0:T(8,128)(2,1)} %bitcast.9), calls=%async_computation.3 | async-start | bytes 4751360 | tf_op jit(solution)/shard_map/all_to_all | solution.py:62
  202.2 32.3 %all-to-all-start.4 = ((bf16[8,40,3584]{2,1,0:T(8,128)(2,1)}), bf16[8,40,3584]{2,1,0:T(8,128)(2,1)S(1)}, u32[]{:S(2)}, u32[]{:S(2)}) async-start(bf16[8,40,3584]{2,1,0:T(8,128)(2,1)} %bitcast.107), calls=%async_computation.6 | async-start | bytes 4587520 | tf_op jit(solution)/shard_map/all_to_all | solution.py:62
  205.8 78.0 %reduce-scatter.7.cloned.1.call-start = ((), (), s32[]{:S(2)}) async-start(), calls=%async_computation.14 | async-start | bytes 1146880 | tf_op jit(solution)/shard_map/reduce_scatter | solution.py:39
  210.4 3.4 %copy-start.4 = (bf16[128,320]{0,1:T(8,128)(2,1)S(1)}, bf16[128,320]{0,1:T(8,128)(2,1)}, u32[]{:S(2)}) copy-start(bf16[128,320]{0,1:T(8,128)(2,1)} %get-tuple-element.31) | copy-start | bytes 245764
  234.5 13.7 %all-to-all-start.5 = ((bf16[8,40,896]{2,1,0:T(8,128)(2,1)}), bf16[8,40,896]{2,1,0:T(8,128)(2,1)S(1)}, u32[]{:S(2)}, u32[]{:S(2)}) async-start(bf16[8,40,896]{2,1,0:T(8,128)(2,1)} %bitcast.113), calls=%async_computation.7 | async-start | bytes 1146880 | tf_op jit(solution)/shard_map/all_to_all | solution.py:62
  248.2 32.3 %all-to-all-start.6 = ((bf16[8,40,3584]{2,1,0:T(8,128)(2,1)}), bf16[8,40,3584]{2,1,0:T(8,128)(2,1)S(1)}, u32[]{:S(2)}, u32[]{:S(2)}) async-start(bf16[8,40,3584]{2,1,0:T(8,128)(2,1)} %bitcast.106), calls=%async_computation.9 | async-start | bytes 4587520 | tf_op jit(solution)/shard_map/all_to_all | solution.py:62
  251.9 33.7 %reduce-scatter.9.cloned.1.call-start = ((), (), s32[]{:S(2)}) async-start(), calls=%async_computation.15 | async-start | bytes 1146880 | tf_op jit(solution)/shard_map/reduce_scatter | solution.py:39
  256.2 51.0 %reduce-scatter.11.cloned.1.call-start = ((), (), s32[]{:S(2)}) async-start(), calls=%async_computation.16 | async-start | bytes 1146880 | tf_op jit(solution)/shard_map/reduce_scatter | solution.py:39
  283.1 24.1 %copy-start.5 = (bf16[128,1792]{1,0:T(8,128)(2,1)S(1)}, bf16[128,1792]{1,0:T(8,128)(2,1)}, u32[]{:S(2)}) copy-start(bf16[128,1792]{1,0:T(8,128)(2,1)} %param.8) | copy-start | bytes 1376260
  283.1 24.1 %copy-start.8 = (f32[1792]{0:T(1024)S(1)}, f32[1792]{0:T(1024)}, u32[]{:S(2)}) copy-start(f32[1792]{0:T(1024)} %param.9) | copy-start | bytes 21508
Sparse Core Ops, SparseCore 0:
  33.9 42.7 all-gather.2
  78.3 48.1 all-gather.4
  167.2 44.2 reduce-scatter.4
  217.4 24.5 reduce-scatter.6
  256.3 24.5 reduce-scatter.8
  283.2 23.8 reduce-scatter.10

commit v3 on v2

--- a/solution.py
+++ b/solution.py
@@ -26,8 +26,6 @@
     slot_total = region_count * capacity
     gate_w, up_w, down_w = w_gate[0], w_up[0], w_down[0]
 
-    near = width_local // 256 * 128
-    far = width_local - near
     share_count = lax.axis_size("local")
 
     def gather(matrix):
@@ -37,10 +35,6 @@
         width = matrix.shape[1] // share_count
         stacked = jnp.stack([matrix[:, z * width:(z + 1) * width] for z in range(share_count)])
         return lax.psum_scatter(stacked, "local", scatter_dimension=0, tiled=False)
-
-    def columns(matrix, start, width):
-        cuts = [lax.slice_in_dim(matrix, z * width_local + start, z * width_local + start + width, axis=1) for z in range(share_count)]
-        return jnp.concatenate(cuts, axis=1)
 
     flat_routes = regions.reshape(-1)
     one_hot = (flat_routes[:, None] == jnp.arange(region_count, dtype=jnp.int32)[None, :]).astype(F32)
@@ -61,29 +55,20 @@
     def exchange(blocks):
         return lax.all_to_all(blocks, "region", split_axis=0, concat_axis=0, tiled=True)
 
-    grad_near = gather(grad_out[:, :near])
-    far_blocks = exchange(pack_rows(grad_out[:, near:])).reshape(slot_total, far)
+    far_blocks = exchange(pack_rows(grad_out)).reshape(slot_total, width_local)
     gain_high, gain_rest = split_weights(norm_gain)
     gain_mid, gain_low = split_weights(norm_gain - gain_high.astype(F32))
     gain_rows = jnp.stack([gain_high, gain_mid, gain_low])
     tokens_cat = jnp.concatenate([tokens, jnp.pad(gain_rows, ((0, 5), (0, 0)))], axis=0)
-    tokens_cat, grad_near = lax.optimization_barrier((tokens_cat, grad_near))
     tokens_full = gather(tokens_cat)
-    near_rows = exchange(pack_rows(grad_near)).reshape(slot_total, share_count * near)
     far_blocks, tokens_full = lax.optimization_barrier((far_blocks, tokens_full))
-    far_rows = gather(far_blocks)
+    rows_grad = gather(far_blocks)
 
     gain_full = jnp.sum(tokens_full[token_count:token_count + 3].astype(F32), axis=0)
     inputs_full = tokens_full[:token_count].astype(F32)
     inv_rms = lax.rsqrt(jnp.sum(inputs_full * inputs_full, axis=1, keepdims=True) / D + 1e-06)
     normed = (inputs_full * inv_rms * gain_full).astype(BF16)
     rows_in = exchange(pack_rows(normed)).reshape(slot_total, D)
-    pieces = []
-    for z in range(share_count):
-        pieces.append(near_rows[:, z * near:(z + 1) * near])
-        pieces.append(far_rows[:, z * far:(z + 1) * far])
-    rows_grad = jnp.concatenate(pieces, axis=1)
-
     gate_pre = dot(rows_in, gate_w)
     up_pre = dot(rows_in, up_w)
     sig_gate = jax.nn.sigmoid(gate_pre)
@@ -93,6 +78,7 @@
     grad_hidden = lax.dot_general(rows_grad, down_w, LAST, preferred_element_type=F32)
     grad_gate = (grad_hidden * up_pre * sig_gate * (1.0 + gate_pre * (1.0 - sig_gate))).astype(BF16)
     grad_up = (grad_hidden * act_gate).astype(BF16)
+    expert_out, grad_gate, grad_up = lax.optimization_barrier((expert_out, grad_gate, grad_up))
     branch_grad = (
         lax.dot_general(grad_gate, gate_w, LAST, preferred_element_type=F32)
         + lax.dot_general(grad_up, up_w, LAST, preferred_element_type=F32)
@@ -111,30 +97,16 @@
     def combined(rows):
         return dot(weight_high, rows) + dot(weight_low, rows)
 
-    out_far = scatter(columns(expert_out, near, far))
-    near_sent = jnp.concatenate([columns(expert_out, 0, near), scalars], axis=1)
-    out_near = send_home(near_sent)
-    early = send_home(columns(branch_grad, 0, near))
-    out_near, out_far = lax.optimization_barrier((out_near, out_far))
-    scalars = out_near[:, share_count * near:]
-    picked = jnp.einsum("tks,sc->tkc", hits.astype(BF16), scalars, preferred_element_type=F32)
+    out_share = scatter(expert_out)
+    back_grad = send_home(jnp.concatenate([branch_grad, scalars], axis=1))
+    picked = jnp.einsum("tks,sc->tkc", hits.astype(BF16), back_grad[:, D:], preferred_element_type=F32)
     picked = lax.psum(picked[:, :, :2] + picked[:, :, 2:4], "local")
     grad_combine = picked[:, :, 0]
     inner = jnp.sum(picked[:, :, 1] * combine, axis=1, keepdims=True) / inv_rms
-
-    moe_near = scatter(combined(out_near[:, :share_count * near]).astype(BF16))
-    out_far, early = lax.optimization_barrier((out_far, early))
-    back_far = send_home(out_far)
-    moe_far = combined(back_far).astype(BF16)
-    moe_out = jnp.concatenate([moe_near, moe_far], axis=1)
-
-    early = combined(early).astype(BF16)
-    late, back_far, early = lax.optimization_barrier((columns(branch_grad, near, far), back_far, early))
-    early = scatter(early)
-    late = send_home(late)
-    late, inner = lax.optimization_barrier((late, inner))
-    late = scatter(combined(late).astype(BF16))
-    grad_normed = jnp.concatenate([early, late], axis=1)
+    grad_sum = combined(back_grad[:, :D]).astype(BF16)
+    grad_sum, out_share = lax.optimization_barrier((grad_sum, out_share))
+    grad_normed = scatter(grad_sum)
+    moe_out = combined(send_home(out_share)).astype(BF16)
     scaled = norm_gain * grad_normed.astype(F32)
     grad_tokens = (
         inv_rms * scaled - tokens.astype(F32) * inv_rms * inv_rms * inv_rms * inner / D

time: 317 us -> 293 us (0.924)
  blocking collectives: 32.5 us -> 148 us
  waiting for transfers between devices: 146 us -> 66.6 us
  starting transfers between devices: 27.9 us -> 4.14 us
  local copies, waits for them, and re-layouts: 20.6 us -> 3.29 us
  matrix products: 52.1 us -> 40.5 us
  other arithmetic: 22.2 us -> 16.2 us
    all_to_all x0 -> x3, blocking collectives: none -> 136 us  [exchange(): lax.all_to_all(blocks, 'region', split_axis=0, concat_axis=0, tiled=True)]
    all_to_all x7 -> x1, waiting for transfers between devices: 64.7 us -> 3.24 us  [exchange(): lax.all_to_all(blocks, 'region', split_axis=0, concat_axis=0, tiled=True)]
    all_to_all x7 -> x1, starting transfers between devices: 27.5 us -> 3.8 us  [exchange(): lax.all_to_all(blocks, 'region', split_axis=0, concat_axis=0, tiled=True)]
    all_gather x1 -> x0, blocking collectives: 22.8 us -> none  [gather(): return lax.all_gather(matrix, 'local', axis=1, tiled=True)]
    all_gather x2, waiting for transfers between devices: 58.8 us -> 40.6 us  [gather(): return lax.all_gather(matrix, 'local', axis=1, tiled=True)]
    dot_general x12 -> x8, matrix products: 24 us -> 14.8 us  [dot(): return jnp.dot(left, right, preferred_element_type=F32)]
    unnamed x45 -> x21, local copies, waits for them, and re-layouts: 10.6 us -> 1.79 us
    dot_general x3 -> x2, matrix products: 8.34 us -> 3.54 us  [pack_rows(): lax.dot_general(spread, matrix, (((0,), (0,)), ((), ())), preferred_eleme...]
  transfers between devices with their start and end apart: 13 -> 5, of which waited for: 10 -> 5; matrix products, arithmetic and copies ran while one was open for 20% -> 13% of each run, Pallas kernels for 0% -> 0%
where the time goes in v3:
time: 293 us; the launch traced here: 292 us
  blocking collectives  148 us (51%)
  waiting for transfers between devices  66.6 us (23%)
  matrix products  40.5 us (14%)
  other arithmetic  16.2 us (6%)
  between operations  14 us (5%)
  starting transfers between devices  4.14 us (1%)
  local copies, waits for them, and re-layouts  3.29 us (1%)
    all_to_all x3, blocking collectives, exchange(): lax.all_to_all(blocks, 'region', split_axis=0, concat_axis=0, tiled=True)  136 us
    all_gather x2, waiting for transfers between devices, gather(): return lax.all_gather(matrix, 'local', axis=1, tiled=True)  40.6 us
    reduce_scatter x2, waiting for transfers between devices, scatter(): return lax.psum_scatter(stacked, 'local', scatter_dimension=0, tiled=False)  22.6 us
    dot_general x8, matrix products, dot(): return jnp.dot(left, right, preferred_element_type=F32)  14.8 us
    psum x1, blocking collectives, on_device(): picked = lax.psum(picked[:, :, :2] + picked[:, :, 2:4], 'local')  11.5 us
    dot_general x1, matrix products, on_device(): lax.dot_general(grad_up, up_w, LAST, preferred_element_type=F32)  7.92 us
    dot_general x1, matrix products, on_device(): lax.dot_general(rows_grad, down_w, LAST, preferred_element_type=F32)  7.37 us
  transfers between devices with their start and end apart: 5, of which 5 were waited for; matrix products, arithmetic and copies ran while one was open for 13% of the time, Pallas kernels for 0%

profile of v3, /device:TPU:0, one launch (start us, length us, event | category | flops | bytes accessed | tf_op | source)
XLA Modules:
  0.0 292.3 jit_solution(16531400507382712446)
XLA Ops:
  7.2 0.0 all-gather.3.cloned.1.call-start
  7.2 0.8 fusion.46
  8.1 1.8 pad_maximum_fusion.2
  9.9 0.0 all-gather.5.cloned.1.call-start
  10.0 0.8 copy.22
  10.8 0.1 eq.28
  10.9 0.2 fusion.25
  11.1 0.1 convert_element_type.126
  11.3 0.1 copy.23
  11.3 0.7 multiply_add_fusion
  12.1 0.8 select_reduce_fusion
  12.8 0.4 convolution_convert_fusion.2
  13.3 21.5 %all_to_all.20 = bf16[8,40,1792]{2,1,0:T(8,128)(2,1)} all-to-all(bf16[8,40,1792]{2,1,0:T(8,128)(2,1)S(1)} %bitcast.72), channel_id=1, replica_groups=mesh['region'=8,'local'=4] {'region'}, dimensions={0} | all-to-all | bytes 2293760 | tf_op jit(solution)/shard_map/all_to_all | solution.py:56
  34.8 21.3 %all-gather.3.cloned.1.call-done = bf16[136,7168]{1,0:T(8,128)(2,1)} async-done(((bf16[136,1792]{1,0:T(8,128)(2,1)}), bf16[136,7168]{1,0:T(8,128)(2,1)}) %all-gather.3.cloned.1.call-update) | async-done | bytes 1949712 | tf_op jit(solution)/shard_map/all_gather | solution.py:32
  56.1 0.0 reduce-scatter.3.cloned.1.call-start
  56.2 2.1 fusion.17
  58.3 1.0 convert_reduce_fusion.1
  59.3 3.1 %convolution_convert_fusion.1 = bf16[320,7168]{1,0:T(8,128)(2,1)S(1)} fusion(f32[7168]{0:T(1024)S(1)} %convert_reduce_fusion.1, f32[128]{0:T(128)S(1)} %fusion.42, bf16[136,7168]{1,0:T(8,128)(2,1)} %all-gather.3.cloned.1.call-done, bf16[128,320]{0,1:T(8,128)(2,1)S(1)} %get-tuple-element.18), kind=kOutput, calls=%fused_computation.3 | convolution fusion | flops 593166336 | bytes 6533632 | tf_op jit(solution)/shard_map/dot_general | solution.py:52
  62.4 57.0 %all_to_all.21 = bf16[8,40,7168]{2,1,0:T(8,128)(2,1)S(1)} all-to-all(bf16[8,40,7168]{2,1,0:T(8,128)(2,1)S(1)} %bitcast.64), channel_id=1, replica_groups=mesh['region'=8,'local'=4] {'region'}, dimensions={0} | all-to-all | bytes 9175040 | tf_op jit(solution)/shard_map/all_to_all | solution.py:56
  119.4 2.5 fusion.7
  121.9 2.5 fusion.11
  124.5 19.3 %all-gather.5.cloned.1.call-done = bf16[320,7168]{1,0:T(8,128)(2,1)} async-done(((bf16[320,1792]{1,0:T(8,128)(2,1)}), bf16[320,7168]{1,0:T(8,128)(2,1)}) %all-gather.5.cloned.1.call-update) | async-done | bytes 4587536 | tf_op jit(solution)/shard_map/all_gather | solution.py:32
  143.8 7.4 %multiply_reduce_fusion = (f32[320]{0:T(512)S(1)}, bf16[320,512]{1,0:T(8,128)(2,1)S(1)}, bf16[320,512]{1,0:T(8,128)(2,1)S(1)}, bf16[320,512]{1,0:T(8,128)(2,1)S(1)}) fusion(f32[320,512]{1,0:T(8,128)S(1)} %fusion.7, f32[320,512]{1,0:T(8,128)S(1)} %fusion.11, bf16[320,7168]{1,0:T(8,128)(2,1)} %all-gather.5.cloned.1.call-done, bf16[1,512,7168]{2,1,0:T(8,128)(2,1)} %param.12), kind=kOutput, calls=%fused_computation.46 | convolution fusion | flops 2351759104 | bytes 14222592 | tf_op jit(solution)/shard_map/dot_general | solution.py:78
  151.1 5.6 %convolution_convert_fusion = bf16[320,7168]{1,0:T(8,128)(2,1)S(1)} fusion(bf16[320,512]{1,0:T(8,128)(2,1)S(1)} %get-tuple-element.20, bf16[1,512,7168]{2,1,0:T(8,128)(2,1)} %param.12), kind=kOutput, calls=%fused_computation.2 | convolution fusion | flops 2351104000 | bytes 12255232 | tf_op jit(solution)/shard_map/dot_general | solution.py:13
  156.8 0.3 slice_bitcast_fusion.3
  157.1 2.4 pad_maximum_fusion
  159.6 0.2 reduce-scatter.5.cloned.1.call-start
  159.8 0.2 add_reduce_fusion
  160.1 0.2 copy.24
  160.3 5.8 %fusion.9 = f32[320,7168]{1,0:T(8,128)S(1)} fusion(bf16[320,512]{1,0:T(8,128)(2,1)S(1)} %get-tuple-element.12, bf16[1,7168,512]{2,1,0:T(8,128)(2,1)} %param.10), kind=kOutput, calls=%fused_computation.14 | convolution fusion | flops 2348810240 | bytes 16842752 | tf_op jit(solution)/shard_map/dot_general | solution.py:83
  166.0 7.9 %fusion = bf16[320,7168]{1,0:T(8,128)(2,1)} fusion(f32[320,7168]{1,0:T(8,128)S(1)} %fusion.9, bf16[320,512]{1,0:T(8,128)(2,1)S(1)} %get-tuple-element.13, bf16[1,7168,512]{2,1,0:T(8,128)(2,1)} %param.11), kind=kOutput, calls=%fused_computation.1 | convolution fusion | flops 2353397760 | bytes 21430272 | tf_op jit(solution)/shard_map/dot_general | solution.py:84
  173.9 2.6 fusion.13
  176.6 57.6 %all_to_all.22 = bf16[8,40,7296]{2,1,0:T(8,128)(2,1)S(1)} all-to-all(bf16[8,40,7296]{2,1,0:T(8,128)(2,1)S(1)} %bitcast.65), channel_id=1, replica_groups=mesh['region'=8,'local'=4] {'region'}, dimensions={0} | all-to-all | bytes 9338880 | tf_op jit(solution)/shard_map/all_to_all | solution.py:56
  234.2 1.1 fusion.15
  235.3 0.9 copy-done.2
  236.3 1.1 fusion.2
  237.4 3.8 %reduce-scatter.3.cloned.1.call-done = bf16[1,320,1792]{2,1,0:T(8,128)(2,1)} async-done(((bf16[4,320,1792]{2,1,0:T(8,128)(2,1)}), bf16[1,320,1792]{2,1,0:T(8,128)(2,1)}) %reduce-scatter.3.cloned.1.call-update) | async-done | bytes 1146896 | tf_op jit(solution)/shard_map/reduce_scatter | solution.py:37
  241.3 0.1 slice_bitcast_fusion.7
  241.4 1.5 pad_maximum_fusion.1
  242.9 3.8 %all-to-all-start.3 = ((bf16[8,40,1792]{2,1,0:T(8,128)(2,1)}), bf16[8,40,1792]{2,1,0:T(8,128)(2,1)S(1)}, u32[]{:S(2)}, u32[]{:S(2)}) async-start(bf16[8,40,1792]{2,1,0:T(8,128)(2,1)} %bitcast.76), calls=%async_computation.4 | async-start | bytes 2293760 | tf_op jit(solution)/shard_map/all_to_all | solution.py:56
  246.7 1.1 fusion.30
  247.9 11.5 %psum.7 = f32[128,2,2]{0,2,1:T(2,128)S(1)} all-reduce(f32[128,2,2]{0,2,1:T(2,128)S(1)} %slice_add_fusion), channel_id=1, replica_groups=mesh['region'=8,'local'=4] {'local'}, use_global_device_ids=true, to_apply=%region_9.10 | all-reduce | flops 512 | bytes 4096 | tf_op jit(solution)/shard_map/psum | solution.py:103
  259.4 0.6 fusion.47
  260.0 3.2 %all-to-all-done.3 = bf16[8,40,1792]{2,1,0:T(8,128)(2,1)S(1)} async-done(((bf16[8,40,1792]{2,1,0:T(8,128)(2,1)}), bf16[8,40,1792]{2,1,0:T(8,128)(2,1)S(1)}, u32[]{:S(2)}, u32[]{:S(2)}) %all-to-all-start.3) | async-done | bytes 1146912 | tf_op jit(solution)/shard_map/all_to_all | solution.py:56
  263.2 0.4 fusion.43
  263.6 1.2 fusion.20
  264.8 18.8 %reduce-scatter.5.cloned.1.call-done = bf16[1,128,1792]{2,1,0:T(8,128)(2,1)} async-done(((bf16[4,128,1792]{2,1,0:T(8,128)(2,1)}), bf16[1,128,1792]{2,1,0:T(8,128)(2,1)}) %reduce-scatter.5.cloned.1.call-update) | async-done | bytes 458768 | tf_op jit(solution)/shard_map/reduce_scatter | solution.py:37
  283.6 2.1 fusion.28
  (39 shorter events, 0.3 us)
Async XLA Ops:
  7.2 5.7 %copy-start = (bf16[128,1792]{1,0:T(8,128)(2,1)S(1)}, bf16[128,1792]{1,0:T(8,128)(2,1)}, u32[]{:S(2)}) copy-start(bf16[128,1792]{1,0:T(8,128)(2,1)} %param.15) | copy-start | bytes 1376260
  7.2 48.9 %all-gather.3.cloned.1.call-start = ((), (), s32[]{:S(2)}) async-start(), calls=%async_computation.6 | async-start | bytes 2437120 | tf_op jit(solution)/shard_map/all_gather | solution.py:32
  9.9 133.8 %all-gather.5.cloned.1.call-start = ((), (), s32[]{:S(2)}) async-start(), calls=%async_computation.7 | async-start | bytes 5734400 | tf_op jit(solution)/shard_map/all_gather | solution.py:32
  56.1 185.2 %reduce-scatter.3.cloned.1.call-start = ((), (), s32[]{:S(2)}) async-start(), calls=%async_computation.8 | async-start | bytes 5734400 | tf_op jit(solution)/shard_map/reduce_scatter | solution.py:37
  56.2 63.2 %slice-start.2 = ((s8[7340032]{0:T(1024)(128)(4,1)}), s8[4194304]{0:T(1024)(128)(4,1)S(1)}, s32[]{:S(2)}) async-start(s8[7340032]{0:T(1024)(128)(4,1)} %bitcast.70), calls=%async_computation.12 | async-start | bytes 8388608
  59.3 60.1 %slice-start.3 = ((s8[7340032]{0:T(1024)(128)(4,1)}), s8[3145728]{0:T(1024)(128)(4,1)S(1)}, s32[]{:S(2)}) async-start(s8[7340032]{0:T(1024)(128)(4,1)} %bitcast.70), calls=%async_computation.13 | async-start | bytes 6291456
  62.4 59.5 %slice-start = ((s8[7340032]{0:T(1024)(128)(4,1)}), s8[3145728]{0:T(1024)(128)(4,1)S(1)}, s32[]{:S(2)}) async-start(s8[7340032]{0:T(1024)(128)(4,1)} %bitcast.68), calls=%async_computation.10 | async-start | bytes 6291456
  119.4 2.5 slice-start.1
  159.6 124.1 %reduce-scatter.5.cloned.1.call-start = ((), (), s32[]{:S(2)}) async-start(), calls=%async_computation.9 | async-start | bytes 2293760 | tf_op jit(solution)/shard_map/reduce_scatter | solution.py:37
  234.2 2.1 copy-start.2
  241.4 18.5 %copy-start.5 = (f32[128,2]{0,1:T(2,128)S(1)}, f32[128,2]{0,1:T(2,128)}, u32[]{:S(2)}) copy-start(f32[128,2]{0,1:T(2,128)} %param.14) | copy-start | bytes 3076
  242.9 40.7 %copy-start.3 = (bf16[128,1792]{1,0:T(8,128)(2,1)S(1)}, bf16[128,1792]{1,0:T(8,128)(2,1)}, u32[]{:S(2)}) copy-start(bf16[128,1792]{1,0:T(8,128)(2,1)} %param.8) | copy-start | bytes 1376260
  242.9 40.7 %copy-start.4 = (f32[1792]{0:T(1024)S(1)}, f32[1792]{0:T(1024)}, u32[]{:S(2)}) copy-start(f32[1792]{0:T(1024)} %param.9) | copy-start | bytes 21508
  242.9 42.9 %copy-start.1 = (bf16[128,1792]{1,0:T(8,128)(2,1)S(1)}, bf16[128,1792]{1,0:T(8,128)(2,1)}, u32[]{:S(2)}) copy-start(bf16[128,1792]{1,0:T(8,128)(2,1)} %param.15) | copy-start | bytes 1376260
  242.9 20.3 %all-to-all-start.3 = ((bf16[8,40,1792]{2,1,0:T(8,128)(2,1)}), bf16[8,40,1792]{2,1,0:T(8,128)(2,1)S(1)}, u32[]{:S(2)}, u32[]{:S(2)}) async-start(bf16[8,40,1792]{2,1,0:T(8,128)(2,1)} %bitcast.76), calls=%async_computation.4 | async-start | bytes 2293760 | tf_op jit(solution)/shard_map/all_to_all | solution.py:56
Sparse Core Ops, SparseCore 0:
  10.1 45.9 all-gather.2
  57.7 86.0 all-gather.4
  159.7 81.5 reduce-scatter.2
  243.4 40.1 reduce-scatter.4

commit v4 on v3

--- a/solution.py
+++ b/solution.py
@@ -1,6 +1,10 @@
+import functools
+
 import jax
 import jax.numpy as jnp
 from jax import lax
+from jax.experimental import pallas as pl
+from jax.experimental.pallas import tpu as pltpu
 from jax.sharding import PartitionSpec as P
 
 D = 7168
@@ -16,6 +20,110 @@
 def split_weights(weights):
     high = weights.astype(BF16)
     return high, (weights - high.astype(F32)).astype(BF16)
+
+
+def spread_kernel(share, regions, near_ref, far_ref, near_out, far_out, up_send, up_recv, down_send, down_recv, far_send, far_recv, own_sem):
+    region, z = lax.axis_index("region"), lax.axis_index("local")
+    width = near_ref.shape[1]
+    has_above, has_below = z + 1 < share, z >= 1
+
+    barrier = pltpu.get_barrier_semaphore()
+
+    def greet(there):
+        pl.semaphore_signal(barrier, inc=1, device_id=there, device_id_type=pl.DeviceIdType.MESH)
+
+    for offset in range(1, regions):
+        greet((lax.rem(region + offset, regions), z))
+    pl.when(has_above)(lambda: greet((region, z + 1)))
+    pl.when(has_below)(lambda: greet((region, z - 1)))
+    inside = has_above & has_below
+    pl.when(inside)(lambda: pl.semaphore_wait(barrier, regions + 1))
+    pl.when(jnp.logical_not(inside))(lambda: pl.semaphore_wait(barrier, regions))
+
+    def slot(owner):
+        return near_out.at[:, pl.ds(pl.multiple_of(owner * width, 128), width)]
+
+    def hop(step, way):
+        owner = z - step * way
+        send, recv = (up_send, up_recv) if way > 0 else (down_send, down_recv)
+        return pltpu.make_async_remote_copy(
+            src_ref=near_ref if step == 0 else slot(owner),
+            dst_ref=slot(owner),
+            send_sem=send.at[step],
+            recv_sem=recv.at[step],
+            device_id=(region, z + way),
+            device_id_type=pl.DeviceIdType.MESH,
+        )
+
+    def landed(step, way):
+        owner = z - (step + 1) * way
+        send, recv = (up_send, up_recv) if way > 0 else (down_send, down_recv)
+        pltpu.make_async_remote_copy(
+            src_ref=slot(owner),
+            dst_ref=slot(owner),
+            send_sem=send.at[step],
+            recv_sem=recv.at[step],
+            device_id=(region, z + way),
+            device_id_type=pl.DeviceIdType.MESH,
+        ).wait_recv()
+
+    def sends(step, way):
+        owner = z - step * way
+        there = has_above if way > 0 else has_below
+        return there & (owner >= 0) & (owner < share)
+
+    def parcel(offset):
+        peer = lax.rem(region + offset, regions)
+        return pltpu.make_async_remote_copy(
+            src_ref=far_ref.at[peer],
+            dst_ref=far_out.at[region],
+            send_sem=far_send.at[offset],
+            recv_sem=far_recv.at[offset],
+            device_id=(peer, z),
+            device_id_type=pl.DeviceIdType.MESH,
+        )
+
+    for way in (1, -1):
+        pl.when(sends(0, way))(lambda way=way: hop(0, way).start())
+    for offset in range(1, regions):
+        parcel(offset).start()
+    own_near = pltpu.make_async_copy(near_ref, slot(z), own_sem.at[0])
+    own_far = pltpu.make_async_copy(far_ref.at[region], far_out.at[region], own_sem.at[1])
+    own_near.start()
+    own_far.start()
+    for step in range(1, share):
+        for way in (1, -1):
+            owner = z - step * way
+            pl.when((owner >= 0) & (owner < share))(lambda step=step, way=way: landed(step - 1, way))
+            if step < share - 1:
+                pl.when(sends(step, way))(lambda step=step, way=way: hop(step, way).start())
+    for step in range(share - 1):
+        for way in (1, -1):
+            pl.when(sends(step, way))(lambda step=step, way=way: hop(step, way).wait_send())
+    for offset in range(1, regions):
+        parcel(offset).wait()
+    own_near.wait()
+    own_far.wait()
+
+
+def spread_out(number, near, far):
+    share, regions = lax.axis_size("local"), lax.axis_size("region")
+    rows, width = near.shape
+    moved = 2 * (rows * width * share + 2 * far.size)
+    return pl.pallas_call(
+        functools.partial(spread_kernel, share, regions),
+        out_shape=(
+            jax.ShapeDtypeStruct((rows, width * share), near.dtype),
+            jax.ShapeDtypeStruct(far.shape, far.dtype),
+        ),
+        in_specs=[pl.BlockSpec(memory_space=pl.ANY)] * 2,
+        out_specs=[pl.BlockSpec(memory_space=pl.ANY)] * 2,
+        scratch_shapes=[pltpu.SemaphoreType.DMA((share,))] * 4
+        + [pltpu.SemaphoreType.DMA((regions,))] * 2
+        + [pltpu.SemaphoreType.DMA((2,))],
+        compiler_params=pltpu.CompilerParams(collective_id=number, has_side_effects=True),
+        cost_estimate=pl.CostEstimate(flops=0, bytes_accessed=moved, transcendentals=0),
+    )(near, far)
 
 
 def on_device(tokens, norm_gain, w_gate, w_up, w_down, regions, combine, grad_out):
@@ -27,9 +135,6 @@
     gate_w, up_w, down_w = w_gate[0], w_up[0], w_down[0]
 
     share_count = lax.axis_size("local")
-
-    def gather(matrix):
-        return lax.all_gather(matrix, "local", axis=1, tiled=True)
 
     def scatter(matrix):
         width = matrix.shape[1] // share_count
@@ -55,20 +160,18 @@
     def exchange(blocks):
         return lax.all_to_all(blocks, "region", split_axis=0, concat_axis=0, tiled=True)
 
-    far_blocks = exchange(pack_rows(grad_out)).reshape(slot_total, width_local)
     gain_high, gain_rest = split_weights(norm_gain)
     gain_mid, gain_low = split_weights(norm_gain - gain_high.astype(F32))
     gain_rows = jnp.stack([gain_high, gain_mid, gain_low])
-    tokens_cat = jnp.concatenate([tokens, jnp.pad(gain_rows, ((0, 5), (0, 0)))], axis=0)
-    tokens_full = gather(tokens_cat)
-    far_blocks, tokens_full = lax.optimization_barrier((far_blocks, tokens_full))
-    rows_grad = gather(far_blocks)
+    tokens_cat = jnp.concatenate([tokens, jnp.pad(gain_rows, ((0, 13), (0, 0)))], axis=0)
+    tokens_full, far_blocks = spread_out(0, tokens_cat, pack_rows(grad_out))
 
     gain_full = jnp.sum(tokens_full[token_count:token_count + 3].astype(F32), axis=0)
     inputs_full = tokens_full[:token_count].astype(F32)
     inv_rms = lax.rsqrt(jnp.sum(inputs_full * inputs_full, axis=1, keepdims=True) / D + 1e-06)
     normed = (inputs_full * inv_rms * gain_full).astype(BF16)
-    rows_in = exchange(pack_rows(normed)).reshape(slot_total, D)
+    rows_grad, rows_in = spread_out(1, far_blocks.reshape(slot_total, width_local), pack_rows(normed))
+    rows_in = rows_in.reshape(slot_total, D)
     gate_pre = dot(rows_in, gate_w)
     up_pre = dot(rows_in, up_w)
     sig_gate = jax.nn.sigmoid(gate_pre)

time: 293 us -> 303 us (1.034)
  Pallas kernels: 0 us -> 123 us
  blocking collectives: 148 us -> 69.3 us
  waiting for transfers between devices: 66.6 us -> 27.5 us
  matrix products: 40.5 us -> 44.2 us
    pallas_call x0 -> x2, Pallas kernels: none -> 123 us  [spread_out(): pl.pallas_call(functools.partial(spread_kernel, share, regions), out_shap...]
    all_to_all x3 -> x1, blocking collectives: 136 us -> 57.8 us  [exchange(): lax.all_to_all(blocks, 'region', split_axis=0, concat_axis=0, tiled=True)]
    all_gather x2 -> x0, waiting for transfers between devices: 40.6 us -> none  [gather(): return lax.all_gather(matrix, 'local', axis=1, tiled=True)]
    dot_general x8, matrix products: 14.8 us -> 19.6 us  [dot(): return jnp.dot(left, right, preferred_element_type=F32)]
    dot_general x1, matrix products: 7.37 us -> 2.88 us  [on_device(): lax.dot_general(rows_grad, down_w, LAST, preferred_element_type=F32)]
  transfers between devices with their start and end apart: 5 -> 3, of which waited for: 5 -> 3; matrix products, arithmetic and copies ran while one was open for 13% -> 8% of each run, Pallas kernels for 0% -> 0%
where the time goes in v4:
time: 303 us; the launch traced here: 302 us
  Pallas kernels  123 us (41%)
  blocking collectives  69.3 us (23%)
  matrix products  44.2 us (15%)
  waiting for transfers between devices  27.5 us (9%)
  other arithmetic  16.1 us (5%)
  between operations  14.4 us (5%)
  starting transfers between devices  4.11 us (1%)
  local copies, waits for them, and re-layouts  3.29 us (1%)
    pallas_call x2, Pallas kernels, spread_out(): pl.pallas_call(functools.partial(spread_kernel, share, regions), out_shap...  123 us
    all_to_all x1, blocking collectives, exchange(): lax.all_to_all(blocks, 'region', split_axis=0, concat_axis=0, tiled=True)  57.8 us
    reduce_scatter x2, waiting for transfers between devices, scatter(): return lax.psum_scatter(stacked, 'local', scatter_dimension=0, tiled=False)  24.2 us
    dot_general x8, matrix products, dot(): return jnp.dot(left, right, preferred_element_type=F32)  19.6 us
    psum x1, blocking collectives, on_device(): picked = lax.psum(picked[:, :, :2] + picked[:, :, 2:4], 'local')  11.5 us
    dot_general x1, matrix products, on_device(): lax.dot_general(grad_up, up_w, LAST, preferred_element_type=F32)  8.41 us
    dot_general x2, matrix products, pack_rows(): lax.dot_general(spread, matrix, (((0,), (0,)), ((), ())), preferred_eleme...  6.44 us
  transfers between devices with their start and end apart: 3, of which 3 were waited for; matrix products, arithmetic and copies ran while one was open for 8% of the time, Pallas kernels for 0%

profile of v4, /device:TPU:0, one launch (start us, length us, event | category | flops | bytes accessed | tf_op | source)
XLA Modules:
  0.0 302.1 jit_solution(1340141246152759466)
XLA Ops:
  7.2 0.0 copy-start
  7.2 0.0 reduce-scatter.3.cloned.1.call-start
  7.2 0.8 fusion.46
  8.0 0.8 copy.22
  8.8 0.1 eq.28
  9.0 0.2 fusion.25
  9.2 0.1 convert_element_type.126
  9.3 0.1 copy.23
  9.4 0.7 multiply_add_fusion
  10.1 0.8 select_reduce_fusion
  10.9 1.9 pad_maximum_fusion.2.near_ref
  12.8 1.4 convolution_convert_fusion.2
  14.2 44.5 %shard_map.103 = (bf16[144,7168]{1,0:T(8,128)(2,1)}, bf16[8,40,1792]{2,1,0:T(8,128)(2,1)}) custom-call(bf16[144,1792]{1,0:T(8,128)(2,1)} %pad_maximum_fusion.2.near_ref, bf16[8,40,1792]{2,1,0:T(8,128)(2,1)} %bitcast.68), custom_call_target="tpu_custom_call" | custom-call | bytes 4358144 | tf_op jit(solution)/shard_map/pallas_call | solution.py:113
  58.7 1.9 fusion.17
  60.6 1.0 convert_reduce_fusion.1
  61.6 5.0 %convolution_convert_fusion.1 = bf16[320,7168]{1,0:T(8,128)(2,1)} fusion(f32[7168]{0:T(1024)S(1)} %convert_reduce_fusion.1, f32[128]{0:T(128)S(1)} %fusion.42, bf16[144,7168]{1,0:T(8,128)(2,1)} %get-tuple-element.13, bf16[128,320]{0,1:T(8,128)(2,1)S(1)} %get-tuple-element.22), kind=kOutput, calls=%fused_computation.3 | convolution fusion | flops 593166336 | bytes 6533632 | tf_op jit(solution)/shard_map/dot_general | solution.py:157
  66.6 78.8 %shard_map.104 = (bf16[320,7168]{1,0:T(8,128)(2,1)}, bf16[8,40,7168]{2,1,0:T(8,128)(2,1)}) custom-call(bf16[320,1792]{1,0:T(8,128)(2,1)} %bitcast.70, bf16[8,40,7168]{2,1,0:T(8,128)(2,1)} %bitcast.64), custom_call_target="tpu_custom_call" | custom-call | bytes 13762560 | tf_op jit(solution)/shard_map/pallas_call | solution.py:113
  145.4 7.1 %fusion.7 = f32[320,512]{1,0:T(8,128)S(1)} fusion(bf16[320,7168]{1,0:T(8,128)(2,1)} %bitcast.77, bf16[1,7168,512]{2,1,0:T(8,128)(2,1)} %param.11), kind=kOutput, calls=%fused_computation.12 | convolution fusion | flops 2348810240 | bytes 12582912 | tf_op jit(solution)/shard_map/dot_general | solution.py:17
  152.6 0.0 slice-start.1
  152.6 5.8 %fusion.11 = f32[320,512]{1,0:T(8,128)S(1)} fusion(bf16[320,7168]{1,0:T(8,128)(2,1)S(1)} %bitcast.78, bf16[1,7168,512]{2,1,0:T(8,128)(2,1)} %param.10), kind=kOutput, calls=%fused_computation.16 | convolution fusion | flops 2348810240 | bytes 12582912 | tf_op jit(solution)/shard_map/dot_general | solution.py:17
  158.4 2.9 multiply_reduce_fusion
  161.3 2.6 convolution_convert_fusion
  163.9 0.3 slice_bitcast_fusion.3
  164.2 2.4 pad_maximum_fusion
  166.6 0.0 reduce-scatter.3.cloned.1.call-update
  166.6 0.3 reduce-scatter.5.cloned.1.call-start
  166.9 0.2 add_reduce_fusion
  167.2 0.2 copy.24
  167.4 5.8 %fusion.9 = f32[320,7168]{1,0:T(8,128)S(1)} fusion(bf16[320,512]{1,0:T(8,128)(2,1)S(1)} %get-tuple-element.16, bf16[1,7168,512]{2,1,0:T(8,128)(2,1)} %param.10), kind=kOutput, calls=%fused_computation.14 | convolution fusion | flops 2348810240 | bytes 16842752 | tf_op jit(solution)/shard_map/dot_general | solution.py:186
  173.1 8.4 %fusion = bf16[320,7168]{1,0:T(8,128)(2,1)} fusion(f32[320,7168]{1,0:T(8,128)S(1)} %fusion.9, bf16[320,512]{1,0:T(8,128)(2,1)S(1)} %get-tuple-element.17, bf16[1,7168,512]{2,1,0:T(8,128)(2,1)} %param.11), kind=kOutput, calls=%fused_computation.1 | convolution fusion | flops 2353397760 | bytes 21430272 | tf_op jit(solution)/shard_map/dot_general | solution.py:187
  181.5 2.7 fusion.13
  184.2 57.8 %all_to_all.10 = bf16[8,40,7296]{2,1,0:T(8,128)(2,1)S(1)} all-to-all(bf16[8,40,7296]{2,1,0:T(8,128)(2,1)S(1)} %bitcast.65), channel_id=1, replica_groups=mesh['region'=8,'local'=4] {'region'}, dimensions={0} | all-to-all | bytes 9338880 | tf_op jit(solution)/shard_map/all_to_all | solution.py:161
  242.0 1.1 fusion.15
  243.2 0.9 copy-done.2
  244.1 1.2 fusion.2
  245.3 5.3 %reduce-scatter.3.cloned.1.call-done = bf16[1,320,1792]{2,1,0:T(8,128)(2,1)} async-done(((bf16[4,320,1792]{2,1,0:T(8,128)(2,1)}), bf16[1,320,1792]{2,1,0:T(8,128)(2,1)}) %reduce-scatter.3.cloned.1.call-update) | async-done | bytes 1146896 | tf_op jit(solution)/shard_map/reduce_scatter | solution.py:142
  250.6 0.1 slice_bitcast_fusion.7
  250.7 1.5 pad_maximum_fusion.1
  252.2 0.0 reduce-scatter.5.cloned.1.call-update
  252.3 3.8 %all-to-all-start.1 = ((bf16[8,40,1792]{2,1,0:T(8,128)(2,1)}), bf16[8,40,1792]{2,1,0:T(8,128)(2,1)S(1)}, u32[]{:S(2)}, u32[]{:S(2)}) async-start(bf16[8,40,1792]{2,1,0:T(8,128)(2,1)} %bitcast.69), calls=%async_computation.2 | async-start | bytes 2293760 | tf_op jit(solution)/shard_map/all_to_all | solution.py:161
  256.1 1.1 fusion.30
  257.2 11.5 %psum.7 = f32[128,2,2]{0,2,1:T(2,128)S(1)} all-reduce(f32[128,2,2]{0,2,1:T(2,128)S(1)} %slice_add_fusion), channel_id=1, replica_groups=mesh['region'=8,'local'=4] {'local'}, use_global_device_ids=true, to_apply=%region_9.10 | all-reduce | flops 512 | bytes 4096 | tf_op jit(solution)/shard_map/psum | solution.py:206
  268.6 0.6 fusion.47
  269.3 3.3 %all-to-all-done.1 = bf16[8,40,1792]{2,1,0:T(8,128)(2,1)S(1)} async-done(((bf16[8,40,1792]{2,1,0:T(8,128)(2,1)}), bf16[8,40,1792]{2,1,0:T(8,128)(2,1)S(1)}, u32[]{:S(2)}, u32[]{:S(2)}) %all-to-all-start.1) | async-done | bytes 1146912 | tf_op jit(solution)/shard_map/all_to_all | solution.py:161
  272.5 0.4 fusion.43
  273.0 1.2 fusion.20
  274.2 18.9 %reduce-scatter.5.cloned.1.call-done = bf16[1,128,1792]{2,1,0:T(8,128)(2,1)} async-done(((bf16[4,128,1792]{2,1,0:T(8,128)(2,1)}), bf16[1,128,1792]{2,1,0:T(8,128)(2,1)}) %reduce-scatter.5.cloned.1.call-update) | async-done | bytes 458768 | tf_op jit(solution)/shard_map/reduce_scatter | solution.py:142
  293.1 2.1 fusion.28
  (35 shorter events, 0.2 us)
Async XLA Ops:
  7.2 5.6 %copy-start = (bf16[128,1792]{1,0:T(8,128)(2,1)S(1)}, bf16[128,1792]{1,0:T(8,128)(2,1)}, u32[]{:S(2)}) copy-start(bf16[128,1792]{1,0:T(8,128)(2,1)} %param.15) | copy-start | bytes 1376260
  7.2 243.4 %reduce-scatter.3.cloned.1.call-start = ((), (), s32[]{:S(2)}) async-start(), calls=%async_computation.4 | async-start | bytes 5734400 | tf_op jit(solution)/shard_map/reduce_scatter | solution.py:142
  145.4 7.2 %copy-start.6 = (bf16[8,40,7168]{2,1,0:T(8,128)(2,1)S(1)}, bf16[8,40,7168]{2,1,0:T(8,128)(2,1)}, u32[]{:S(2)}) copy-start(bf16[8,40,7168]{2,1,0:T(8,128)(2,1)} %get-tuple-element.14) | copy-start | bytes 13762564
  145.4 13.0 %slice-start = ((s8[7340032]{0:T(1024)(128)(4,1)}), s8[4194304]{0:T(1024)(128)(4,1)S(1)}, s32[]{:S(2)}) async-start(s8[7340032]{0:T(1024)(128)(4,1)} %bitcast.73), calls=%async_computation.6 | async-start | bytes 8388608
  145.4 13.0 %slice-start.2 = ((s8[4587520]{0:T(1024)(128)(4,1)}), s8[4194304]{0:T(1024)(128)(4,1)S(1)}, s32[]{:S(2)}) async-start(s8[4587520]{0:T(1024)(128)(4,1)} %bitcast.75), calls=%async_computation.8 | async-start | bytes 8388608
  152.6 5.8 %slice-start.1 = ((s8[7340032]{0:T(1024)(128)(4,1)}), s8[3145728]{0:T(1024)(128)(4,1)S(1)}, s32[]{:S(2)}) async-start(s8[7340032]{0:T(1024)(128)(4,1)} %bitcast.73), calls=%async_computation.7 | async-start | bytes 6291456
  152.6 5.8 %slice-start.3 = ((s8[4587520]{0:T(1024)(128)(4,1)}), s8[393216]{0:T(1024)(128)(4,1)S(1)}, s32[]{:S(2)}) async-start(s8[4587520]{0:T(1024)(128)(4,1)} %bitcast.75), calls=%async_computation.9 | async-start | bytes 786432
  166.6 126.5 %reduce-scatter.5.cloned.1.call-start = ((), (), s32[]{:S(2)}) async-start(), calls=%async_computation.5 | async-start | bytes 2293760 | tf_op jit(solution)/shard_map/reduce_scatter | solution.py:142
  242.0 2.1 copy-start.2
  250.7 18.5 %copy-start.5 = (f32[128,2]{0,1:T(2,128)S(1)}, f32[128,2]{0,1:T(2,128)}, u32[]{:S(2)}) copy-start(f32[128,2]{0,1:T(2,128)} %param.14) | copy-start | bytes 3076
  252.2 40.9 %copy-start.3 = (bf16[128,1792]{1,0:T(8,128)(2,1)S(1)}, bf16[128,1792]{1,0:T(8,128)(2,1)}, u32[]{:S(2)}) copy-start(bf16[128,1792]{1,0:T(8,128)(2,1)} %param.8) | copy-start | bytes 1376260
  252.2 40.9 %copy-start.4 = (f32[1792]{0:T(1024)S(1)}, f32[1792]{0:T(1024)}, u32[]{:S(2)}) copy-start(f32[1792]{0:T(1024)} %param.9) | copy-start | bytes 21508
  252.2 43.0 %copy-start.1 = (bf16[128,1792]{1,0:T(8,128)(2,1)S(1)}, bf16[128,1792]{1,0:T(8,128)(2,1)}, u32[]{:S(2)}) copy-start(bf16[128,1792]{1,0:T(8,128)(2,1)} %param.15) | copy-start | bytes 1376260
  252.3 20.3 %all-to-all-start.1 = ((bf16[8,40,1792]{2,1,0:T(8,128)(2,1)}), bf16[8,40,1792]{2,1,0:T(8,128)(2,1)S(1)}, u32[]{:S(2)}, u32[]{:S(2)}) async-start(bf16[8,40,1792]{2,1,0:T(8,128)(2,1)} %bitcast.69), calls=%async_computation.2 | async-start | bytes 2293760 | tf_op jit(solution)/shard_map/all_to_all | solution.py:161
Sparse Core Ops, SparseCore 0:
  166.7 83.8 reduce-scatter.2
  252.9 40.1 reduce-scatter.4

commit v5 on v3

--- a/solution.py
+++ b/solution.py
@@ -31,9 +31,11 @@
     def gather(matrix):
         return lax.all_gather(matrix, "local", axis=1, tiled=True)
 
-    def scatter(matrix):
+    def stack_shares(matrix):
         width = matrix.shape[1] // share_count
-        stacked = jnp.stack([matrix[:, z * width:(z + 1) * width] for z in range(share_count)])
+        return jnp.stack([matrix[:, z * width:(z + 1) * width] for z in range(share_count)])
+
+    def scatter(stacked):
         return lax.psum_scatter(stacked, "local", scatter_dimension=0, tiled=False)
 
     flat_routes = regions.reshape(-1)
@@ -74,11 +76,11 @@
     sig_gate = jax.nn.sigmoid(gate_pre)
     act_gate = gate_pre * sig_gate
     hidden = (act_gate * up_pre).astype(BF16)
-    expert_out = dot(hidden, down_w).astype(BF16)
+    expert_out = stack_shares(dot(hidden, down_w).astype(BF16))
+    expert_out, rows_grad = lax.optimization_barrier((expert_out, rows_grad))
     grad_hidden = lax.dot_general(rows_grad, down_w, LAST, preferred_element_type=F32)
     grad_gate = (grad_hidden * up_pre * sig_gate * (1.0 + gate_pre * (1.0 - sig_gate))).astype(BF16)
     grad_up = (grad_hidden * act_gate).astype(BF16)
-    expert_out, grad_gate, grad_up = lax.optimization_barrier((expert_out, grad_gate, grad_up))
     branch_grad = (
         lax.dot_general(grad_gate, gate_w, LAST, preferred_element_type=F32)
         + lax.dot_general(grad_up, up_w, LAST, preferred_element_type=F32)
@@ -103,7 +105,7 @@
     picked = lax.psum(picked[:, :, :2] + picked[:, :, 2:4], "local")
     grad_combine = picked[:, :, 0]
     inner = jnp.sum(picked[:, :, 1] * combine, axis=1, keepdims=True) / inv_rms
-    grad_sum = combined(back_grad[:, :D]).astype(BF16)
+    grad_sum = stack_shares(combined(back_grad[:, :D]).astype(BF16))
     grad_sum, out_share = lax.optimization_barrier((grad_sum, out_share))
     grad_normed = scatter(grad_sum)
     moe_out = combined(send_home(out_share)).astype(BF16)

time: 293 us -> 299 us (1.020)
  blocking collectives: 148 us -> 90.5 us
  waiting for transfers between devices: 66.6 us -> 115 us
  matrix products: 40.5 us -> 50.7 us
  starting transfers between devices: 4.14 us -> 8.96 us
    all_to_all x3 -> x2, blocking collectives: 136 us -> 79.1 us  [exchange(): lax.all_to_all(blocks, 'region', split_axis=0, concat_axis=0, tiled=True)]
    all_to_all x1 -> x2, waiting for transfers between devices: 3.24 us -> 55.7 us  [exchange(): lax.all_to_all(blocks, 'region', split_axis=0, concat_axis=0, tiled=True)]
    dot_general x8, matrix products: 14.8 us -> 21.2 us  [dot(): return jnp.dot(left, right, preferred_element_type=F32)]
    all_to_all x1 -> x2, starting transfers between devices: 3.8 us -> 8.39 us  [exchange(): lax.all_to_all(blocks, 'region', split_axis=0, concat_axis=0, tiled=True)]
    all_gather x2, waiting for transfers between devices: 40.6 us -> 37.3 us  [gather(): return lax.all_gather(matrix, 'local', axis=1, tiled=True)]
  transfers between devices with their start and end apart: 5 -> 6, of which waited for: 5 -> 6; matrix products, arithmetic and copies ran while one was open for 13% -> 16% of each run, Pallas kernels for 0% -> 0%
where the time goes in v5:
time: 299 us
  waiting for transfers between devices  115 us (38%)
  blocking collectives  90.5 us (30%)
  matrix products  50.7 us (17%)
  other arithmetic  15.8 us (5%)
  between operations  14 us (5%)
  starting transfers between devices  8.96 us (3%)
  local copies, waits for them, and re-layouts  3.29 us (1%)
    all_to_all x2, blocking collectives, exchange(): lax.all_to_all(blocks, 'region', split_axis=0, concat_axis=0, tiled=True)  79.1 us
    all_to_all x2, waiting for transfers between devices, exchange(): lax.all_to_all(blocks, 'region', split_axis=0, concat_axis=0, tiled=True)  55.7 us
    all_gather x2, waiting for transfers between devices, gather(): return lax.all_gather(matrix, 'local', axis=1, tiled=True)  37.3 us
    reduce_scatter x2, waiting for transfers between devices, scatter(): return lax.psum_scatter(stacked, 'local', scatter_dimension=0, tiled=False)  21.8 us
    dot_general x8, matrix products, dot(): return jnp.dot(left, right, preferred_element_type=F32)  21.2 us
    psum x1, blocking collectives, on_device(): picked = lax.psum(picked[:, :, :2] + picked[:, :, 2:4], 'local')  11.4 us
    all_to_all x2, starting transfers between devices, exchange(): lax.all_to_all(blocks, 'region', split_axis=0, concat_axis=0, tiled=True)  8.39 us
    dot_general x1, matrix products, on_device(): lax.dot_general(grad_up, up_w, LAST, preferred_element_type=F32)  8.29 us
  transfers between devices with their start and end apart: 6, of which 6 were waited for; matrix products, arithmetic and copies ran while one was open for 16% of the time, Pallas kernels for 0%

profile of v5, /device:TPU:0, one launch (start us, length us, event | category | flops | bytes accessed | tf_op | source)
XLA Modules:
  0.0 298.7 jit_solution(6932511514925670180)
XLA Ops:
  7.2 0.8 fusion.46
  8.1 1.9 pad_maximum_fusion.2
  10.0 0.8 copy.22
  10.8 0.1 eq.28
  10.9 0.2 fusion.25
  11.1 0.1 convert_element_type.126
  11.3 0.1 copy.23
  11.3 0.7 multiply_add_fusion
  12.0 0.8 select_reduce_fusion
  12.8 0.4 convolution_convert_fusion.2
  13.2 21.5 %all_to_all.20 = bf16[8,40,1792]{2,1,0:T(8,128)(2,1)} all-to-all(bf16[8,40,1792]{2,1,0:T(8,128)(2,1)S(1)} %bitcast.68), channel_id=1, replica_groups=mesh['region'=8,'local'=4] {'region'}, dimensions={0} | all-to-all | bytes 2293760 | tf_op jit(solution)/shard_map/all_to_all | solution.py:58
  34.7 21.4 %all-gather.3.cloned.1.call-done = bf16[136,7168]{1,0:T(8,128)(2,1)} async-done(((bf16[136,1792]{1,0:T(8,128)(2,1)}), bf16[136,7168]{1,0:T(8,128)(2,1)}) %all-gather.3.cloned.1.call-update) | async-done | bytes 1949712 | tf_op jit(solution)/shard_map/all_gather | solution.py:32
  56.1 1.9 fusion.17
  58.0 1.0 convert_reduce_fusion.1
  59.0 5.1 %convolution_convert_fusion.1 = bf16[320,7168]{1,0:T(8,128)(2,1)} fusion(f32[7168]{0:T(1024)S(1)} %convert_reduce_fusion.1, f32[128]{0:T(128)S(1)} %fusion.42, bf16[136,7168]{1,0:T(8,128)(2,1)} %all-gather.3.cloned.1.call-done, bf16[128,320]{0,1:T(8,128)(2,1)S(1)} %get-tuple-element.18), kind=kOutput, calls=%fused_computation.3 | convolution fusion | flops 593166336 | bytes 6533632 | tf_op jit(solution)/shard_map/dot_general | solution.py:54
  64.2 4.6 %all-to-all-start.1 = ((bf16[8,40,7168]{2,1,0:T(8,128)(2,1)}), bf16[8,40,7168]{2,1,0:T(8,128)(2,1)}, u32[]{:S(2)}, u32[]{:S(2)}) async-start(bf16[8,40,7168]{2,1,0:T(8,128)(2,1)} %bitcast.64), calls=%async_computation.1 | async-start | bytes 9175040 | tf_op jit(solution)/shard_map/all_to_all | solution.py:58
  68.8 0.0 all-gather.5.cloned.1.call-start
  68.8 0.7 all-gather.5.cloned.1.call-update
  69.5 0.2 reduce-scatter.3.cloned.1.call-start
  69.8 52.4 %all-to-all-done.1 = bf16[8,40,7168]{2,1,0:T(8,128)(2,1)} async-done(((bf16[8,40,7168]{2,1,0:T(8,128)(2,1)}), bf16[8,40,7168]{2,1,0:T(8,128)(2,1)}, u32[]{:S(2)}, u32[]{:S(2)}) %all-to-all-start.1) | async-done | bytes 4587552 | tf_op jit(solution)/shard_map/all_to_all | solution.py:58
  122.1 7.2 %fusion.11 = f32[320,512]{1,0:T(8,128)S(1)} fusion(bf16[320,7168]{1,0:T(8,128)(2,1)} %bitcast.3, bf16[1,7168,512]{2,1,0:T(8,128)(2,1)} %param.10), kind=kOutput, calls=%fused_computation.16 | convolution fusion | flops 2348810240 | bytes 12582912 | tf_op jit(solution)/shard_map/dot_general | solution.py:13
  129.3 7.3 %multiply_convert_fusion.2 = (bf16[320,512]{1,0:T(8,128)(2,1)S(1)}, f32[320,512]{1,0:T(8,128)S(1)}) fusion(f32[320,512]{1,0:T(8,128)S(1)} %fusion.11, bf16[320,7168]{1,0:T(8,128)(2,1)} %bitcast.3, bf16[1,7168,512]{2,1,0:T(8,128)(2,1)} %param.11), kind=kOutput, calls=%fused_computation.49 | convolution fusion | flops 2349793280 | bytes 13565952 | tf_op jit(solution)/shard_map/dot_general | solution.py:13
  136.7 2.5 convolution_convert_fusion
  139.3 0.3 slice_bitcast_fusion.3
  139.6 2.4 pad_maximum_fusion
  142.0 15.9 %all-gather.5.cloned.1.call-done = bf16[320,7168]{1,0:T(8,128)(2,1)} async-done(((bf16[320,1792]{1,0:T(8,128)(2,1)}), bf16[320,7168]{1,0:T(8,128)(2,1)}) %all-gather.5.cloned.1.call-update) | async-done | bytes 4587536 | tf_op jit(solution)/shard_map/all_gather | solution.py:32
  157.9 8.2 %multiply_reduce_fusion = (f32[320]{0:T(512)S(1)}, f32[320]{0:T(512)S(1)}, f32[320,512]{1,0:T(8,128)}) fusion(bf16[320,512]{1,0:T(8,128)(2,1)S(1)} %get-tuple-element.32, f32[320,512]{1,0:T(8,128)S(1)} %get-tuple-element.33, f32[320,512]{1,0:T(8,128)S(1)} %fusion.11, bf16[320,7168]{1,0:T(8,128)(2,1)} %all-gather.5.cloned.1.call-done, ...), kind=kOutput, calls=%fused_computation.46 | convolution fusion | flops 2352414208 | bytes 14223872 | tf_op jit(solution)/shard_map/dot_general | solution.py:81
  166.1 0.3 reduce-scatter.5.cloned.1.call-start
  166.4 0.2 copy.24
  166.6 6.3 %fusion.9 = f32[320,7168]{1,0:T(8,128)S(1)} fusion(bf16[1,7168,512]{2,1,0:T(8,128)(2,1)} %param.10, f32[320,512]{1,0:T(8,128)} %copy-done.3, f32[320,512]{1,0:T(8,128)} %get-tuple-element.34, f32[320,512]{1,0:T(8,128)} %copy-done.5), kind=kOutput, calls=%fused_computation.14 | convolution fusion | flops 2350448640 | bytes 18481152 | tf_op jit(solution)/shard_map/dot_general | solution.py:85
  172.9 8.3 %fusion = bf16[320,7168]{1,0:T(8,128)(2,1)} fusion(f32[320,7168]{1,0:T(8,128)S(1)} %fusion.9, bf16[1,7168,512]{2,1,0:T(8,128)(2,1)} %param.11, f32[320,512]{1,0:T(8,128)} %get-tuple-element.34, f32[320,512]{1,0:T(8,128)} %copy-done.3), kind=kOutput, calls=%fused_computation.1 | convolution fusion | flops 2354380800 | bytes 22413312 | tf_op jit(solution)/shard_map/dot_general | solution.py:86
  181.2 2.6 fusion.13
  183.8 57.6 %all_to_all.21 = bf16[8,40,7296]{2,1,0:T(8,128)(2,1)S(1)} all-to-all(bf16[8,40,7296]{2,1,0:T(8,128)(2,1)S(1)} %bitcast.65), channel_id=1, replica_groups=mesh['region'=8,'local'=4] {'region'}, dimensions={0} | all-to-all | bytes 9338880 | tf_op jit(solution)/shard_map/all_to_all | solution.py:58
  241.4 1.2 fusion.15
  242.6 0.9 copy-done.2
  243.5 1.2 fusion.2
  244.7 0.1 slice_bitcast_fusion.7
  244.8 1.5 pad_maximum_fusion.1
  246.3 1.5 reduce-scatter.3.cloned.1.call-done
  247.9 3.8 %all-to-all-start.3 = ((bf16[8,40,1792]{2,1,0:T(8,128)(2,1)}), bf16[8,40,1792]{2,1,0:T(8,128)(2,1)S(1)}, u32[]{:S(2)}, u32[]{:S(2)}) async-start(bf16[8,40,1792]{2,1,0:T(8,128)(2,1)} %bitcast.70), calls=%async_computation.4 | async-start | bytes 2293760 | tf_op jit(solution)/shard_map/all_to_all | solution.py:58
  251.7 1.1 fusion.30
  252.8 11.4 %psum.7 = f32[128,2,2]{0,2,1:T(2,128)S(1)} all-reduce(f32[128,2,2]{0,2,1:T(2,128)S(1)} %slice_add_fusion), channel_id=1, replica_groups=mesh['region'=8,'local'=4] {'local'}, use_global_device_ids=true, to_apply=%region_9.10 | all-reduce | flops 512 | bytes 4096 | tf_op jit(solution)/shard_map/psum | solution.py:105
  264.2 0.6 fusion.47
  264.8 3.3 %all-to-all-done.3 = bf16[8,40,1792]{2,1,0:T(8,128)(2,1)S(1)} async-done(((bf16[8,40,1792]{2,1,0:T(8,128)(2,1)}), bf16[8,40,1792]{2,1,0:T(8,128)(2,1)S(1)}, u32[]{:S(2)}, u32[]{:S(2)}) %all-to-all-start.3) | async-done | bytes 1146912 | tf_op jit(solution)/shard_map/all_to_all | solution.py:58
  268.1 0.4 fusion.43
  268.6 1.2 fusion.20
  269.8 20.3 %reduce-scatter.5.cloned.1.call-done = bf16[1,128,1792]{2,1,0:T(8,128)(2,1)} async-done(((bf16[4,128,1792]{2,1,0:T(8,128)(2,1)}), bf16[1,128,1792]{2,1,0:T(8,128)(2,1)}) %reduce-scatter.5.cloned.1.call-update) | async-done | bytes 458768 | tf_op jit(solution)/shard_map/reduce_scatter | solution.py:39
  290.0 2.1 fusion.28
  (38 shorter events, 0.3 us)
Async XLA Ops:
  7.2 5.6 %copy-start = (bf16[128,1792]{1,0:T(8,128)(2,1)S(1)}, bf16[128,1792]{1,0:T(8,128)(2,1)}, u32[]{:S(2)}) copy-start(bf16[128,1792]{1,0:T(8,128)(2,1)} %param.15) | copy-start | bytes 1376260
  7.2 48.9 %all-gather.3.cloned.1.call-start = ((), (), s32[]{:S(2)}) async-start(), calls=%async_computation.6 | async-start | bytes 2437120 | tf_op jit(solution)/shard_map/all_gather | solution.py:32
  64.2 57.9 %all-to-all-start.1 = ((bf16[8,40,7168]{2,1,0:T(8,128)(2,1)}), bf16[8,40,7168]{2,1,0:T(8,128)(2,1)}, u32[]{:S(2)}, u32[]{:S(2)}) async-start(bf16[8,40,7168]{2,1,0:T(8,128)(2,1)} %bitcast.64), calls=%async_computation.1 | async-start | bytes 9175040 | tf_op jit(solution)/shard_map/all_to_all | solution.py:58
  68.8 89.1 %all-gather.5.cloned.1.call-start = ((), (), s32[]{:S(2)}) async-start(), calls=%async_computation.7 | async-start | bytes 5734400 | tf_op jit(solution)/shard_map/all_gather | solution.py:32
  69.5 178.3 %reduce-scatter.3.cloned.1.call-start = ((), (), s32[]{:S(2)}) async-start(), calls=%async_computation.8 | async-start | bytes 5734400 | tf_op jit(solution)/shard_map/reduce_scatter | solution.py:39
  122.1 14.6 %slice-start = ((s8[7340032]{0:T(1024)(128)(4,1)}), s8[4194304]{0:T(1024)(128)(4,1)S(1)}, s32[]{:S(2)}) async-start(s8[7340032]{0:T(1024)(128)(4,1)} %bitcast.73), calls=%async_computation.10 | async-start | bytes 8388608
  129.3 28.6 %copy-start.3 = (f32[320,512]{1,0:T(8,128)}, f32[320,512]{1,0:T(8,128)S(1)}, u32[]{:S(2)}) copy-start(f32[320,512]{1,0:T(8,128)S(1)} %fusion.11) | copy-start | bytes 1966084
  129.3 7.4 %slice-start.1 = ((s8[7340032]{0:T(1024)(128)(4,1)}), s8[3145728]{0:T(1024)(128)(4,1)S(1)}, s32[]{:S(2)}) async-start(s8[7340032]{0:T(1024)(128)(4,1)} %bitcast.73), calls=%async_computation.11 | async-start | bytes 6291456
  136.7 21.2 %copy-start.5 = (f32[320,512]{1,0:T(8,128)}, f32[320,512]{1,0:T(8,128)S(1)}, u32[]{:S(2)}) copy-start(f32[320,512]{1,0:T(8,128)S(1)} %get-tuple-element.33) | copy-start | bytes 1966084
  166.1 123.9 %reduce-scatter.5.cloned.1.call-start = ((), (), s32[]{:S(2)}) async-start(), calls=%async_computation.9 | async-start | bytes 2293760 | tf_op jit(solution)/shard_map/reduce_scatter | solution.py:39
  241.4 2.1 copy-start.2
  244.8 20.0 %copy-start.7 = (f32[128,2]{0,1:T(2,128)S(1)}, f32[128,2]{0,1:T(2,128)}, u32[]{:S(2)}) copy-start(f32[128,2]{0,1:T(2,128)} %param.14) | copy-start | bytes 3076
  247.8 42.2 %copy-start.4 = (bf16[128,1792]{1,0:T(8,128)(2,1)S(1)}, bf16[128,1792]{1,0:T(8,128)(2,1)}, u32[]{:S(2)}) copy-start(bf16[128,1792]{1,0:T(8,128)(2,1)} %param.8) | copy-start | bytes 1376260
  247.8 42.2 %copy-start.6 = (f32[1792]{0:T(1024)S(1)}, f32[1792]{0:T(1024)}, u32[]{:S(2)}) copy-start(f32[1792]{0:T(1024)} %param.9) | copy-start | bytes 21508
  247.9 44.3 %copy-start.1 = (bf16[128,1792]{1,0:T(8,128)(2,1)S(1)}, bf16[128,1792]{1,0:T(8,128)(2,1)}, u32[]{:S(2)}) copy-start(bf16[128,1792]{1,0:T(8,128)(2,1)} %param.15) | copy-start | bytes 1376260
  247.9 20.3 %all-to-all-start.3 = ((bf16[8,40,1792]{2,1,0:T(8,128)(2,1)}), bf16[8,40,1792]{2,1,0:T(8,128)(2,1)S(1)}, u32[]{:S(2)}, u32[]{:S(2)}) async-start(bf16[8,40,1792]{2,1,0:T(8,128)(2,1)} %bitcast.70), calls=%async_computation.4 | async-start | bytes 2293760 | tf_op jit(solution)/shard_map/all_to_all | solution.py:58
Sparse Core Ops, SparseCore 0:
  10.1 45.9 all-gather.2
  71.2 86.6 all-gather.4
  166.2 81.5 reduce-scatter.2
  250.0 39.9 reduce-scatter.4

commit v6 on v5

--- a/solution.py
+++ b/solution.py
@@ -73,6 +73,7 @@
     rows_in = exchange(pack_rows(normed)).reshape(slot_total, D)
     gate_pre = dot(rows_in, gate_w)
     up_pre = dot(rows_in, up_w)
+    gate_pre, up_pre, rows_grad = lax.optimization_barrier((gate_pre, up_pre, rows_grad))
     sig_gate = jax.nn.sigmoid(gate_pre)
     act_gate = gate_pre * sig_gate
     hidden = (act_gate * up_pre).astype(BF16)

time: 299 us -> 294 us (0.983)
  blocking collectives: 90.5 us -> 147 us
  waiting for transfers between devices: 115 us -> 65.6 us
  matrix products: 50.7 us -> 42.4 us
  starting transfers between devices: 8.96 us -> 4.18 us
    all_to_all x2 -> x3, blocking collectives: 79.1 us -> 136 us  [exchange(): lax.all_to_all(blocks, 'region', split_axis=0, concat_axis=0, tiled=True)]
    all_to_all x2 -> x1, waiting for transfers between devices: 55.7 us -> 3.33 us  [exchange(): lax.all_to_all(blocks, 'region', split_axis=0, concat_axis=0, tiled=True)]
    dot_general x8, matrix products: 21.2 us -> 14.8 us  [dot(): return jnp.dot(left, right, preferred_element_type=F32)]
    all_to_all x2 -> x1, starting transfers between devices: 8.39 us -> 3.8 us  [exchange(): lax.all_to_all(blocks, 'region', split_axis=0, concat_axis=0, tiled=True)]
    all_gather x2, waiting for transfers between devices: 37.3 us -> 40.6 us  [gather(): return lax.all_gather(matrix, 'local', axis=1, tiled=True)]
  transfers between devices with their start and end apart: 6 -> 5, of which waited for: 6 -> 5; matrix products, arithmetic and copies ran while one was open for 16% -> 13% of each run, Pallas kernels for 0% -> 0%
where the time goes in v6:
time: 294 us; the launch traced here: 293 us
  blocking collectives  147 us (50%)
  waiting for transfers between devices  65.6 us (22%)
  matrix products  42.4 us (14%)
  other arithmetic  16.1 us (5%)
  between operations  14.1 us (5%)
  starting transfers between devices  4.18 us (1%)
  local copies, waits for them, and re-layouts  3.34 us (1%)
    all_to_all x3, blocking collectives, exchange(): lax.all_to_all(blocks, 'region', split_axis=0, concat_axis=0, tiled=True)  136 us
    all_gather x2, waiting for transfers between devices, gather(): return lax.all_gather(matrix, 'local', axis=1, tiled=True)  40.6 us
    reduce_scatter x2, waiting for transfers between devices, scatter(): return lax.psum_scatter(stacked, 'local', scatter_dimension=0, tiled=False)  21.6 us
    dot_general x8, matrix products, dot(): return jnp.dot(left, right, preferred_element_type=F32)  14.8 us
    psum x1, blocking collectives, on_device(): picked = lax.psum(picked[:, :, :2] + picked[:, :, 2:4], 'local')  11.4 us
    dot_general x1, matrix products, on_device(): lax.dot_general(grad_up, up_w, LAST, preferred_element_type=F32)  8.41 us
    dot_general x1, matrix products, on_device(): lax.dot_general(rows_grad, down_w, LAST, preferred_element_type=F32)  8.17 us
    dot_general x1, matrix products, on_device(): lax.dot_general(grad_gate, gate_w, LAST, preferred_element_type=F32)  6.34 us
  transfers between devices with their start and end apart: 5, of which 5 were waited for; matrix products, arithmetic and copies ran while one was open for 13% of the time, Pallas kernels for 0%

profile of v6, /device:TPU:0, one launch (start us, length us, event | category | flops | bytes accessed | tf_op | source)
XLA Modules:
  0.0 293.1 jit_solution(2174569089929670337)
XLA Ops:
  7.2 0.0 all-gather.3.cloned.1.call-start
  7.2 0.8 fusion.46
  8.1 1.8 pad_maximum_fusion.2
  9.9 0.0 all-gather.5.cloned.1.call-start
  10.0 0.8 copy.22
  10.8 0.1 eq.28
  10.9 0.2 fusion.25
  11.1 0.1 convert_element_type.126
  11.3 0.1 copy.23
  11.3 0.7 multiply_add_fusion
  12.0 0.8 select_reduce_fusion
  12.8 0.4 convolution_convert_fusion.2
  13.3 21.5 %all_to_all.20 = bf16[8,40,1792]{2,1,0:T(8,128)(2,1)} all-to-all(bf16[8,40,1792]{2,1,0:T(8,128)(2,1)S(1)} %bitcast.70), channel_id=1, replica_groups=mesh['region'=8,'local'=4] {'region'}, dimensions={0} | all-to-all | bytes 2293760 | tf_op jit(solution)/shard_map/all_to_all | solution.py:58
  34.7 21.3 %all-gather.3.cloned.1.call-done = bf16[136,7168]{1,0:T(8,128)(2,1)} async-done(((bf16[136,1792]{1,0:T(8,128)(2,1)}), bf16[136,7168]{1,0:T(8,128)(2,1)}) %all-gather.3.cloned.1.call-update) | async-done | bytes 1949712 | tf_op jit(solution)/shard_map/all_gather | solution.py:32
  56.1 0.0 reduce-scatter.3.cloned.1.call-start
  56.2 2.1 fusion.17
  58.3 1.0 convert_reduce_fusion.1
  59.3 3.1 %convolution_convert_fusion.1 = bf16[320,7168]{1,0:T(8,128)(2,1)S(1)} fusion(f32[7168]{0:T(1024)S(1)} %convert_reduce_fusion.1, f32[128]{0:T(128)S(1)} %fusion.42, bf16[136,7168]{1,0:T(8,128)(2,1)} %all-gather.3.cloned.1.call-done, bf16[128,320]{0,1:T(8,128)(2,1)S(1)} %get-tuple-element.24), kind=kOutput, calls=%fused_computation.3 | convolution fusion | flops 593166336 | bytes 6533632 | tf_op jit(solution)/shard_map/dot_general | solution.py:54
  62.4 57.0 %all_to_all.21 = bf16[8,40,7168]{2,1,0:T(8,128)(2,1)S(1)} all-to-all(bf16[8,40,7168]{2,1,0:T(8,128)(2,1)S(1)} %bitcast.62), channel_id=1, replica_groups=mesh['region'=8,'local'=4] {'region'}, dimensions={0} | all-to-all | bytes 9175040 | tf_op jit(solution)/shard_map/all_to_all | solution.py:58
  119.4 2.5 fusion.7
  121.9 2.5 fusion.11
  124.5 19.3 %all-gather.5.cloned.1.call-done = bf16[320,7168]{1,0:T(8,128)(2,1)} async-done(((bf16[320,1792]{1,0:T(8,128)(2,1)}), bf16[320,7168]{1,0:T(8,128)(2,1)}) %all-gather.5.cloned.1.call-update) | async-done | bytes 4587536 | tf_op jit(solution)/shard_map/all_gather | solution.py:32
  143.8 0.2 multiply_convert_fusion.2
  144.0 5.6 %convolution_convert_fusion = bf16[320,7168]{1,0:T(8,128)(2,1)S(1)} fusion(bf16[320,512]{1,0:T(8,128)(2,1)S(1)} %multiply_convert_fusion.2, bf16[1,512,7168]{2,1,0:T(8,128)(2,1)} %param.12), kind=kOutput, calls=%fused_computation.2 | convolution fusion | flops 2351104000 | bytes 12255232 | tf_op jit(solution)/shard_map/dot_general | solution.py:13
  149.6 0.3 slice_bitcast_fusion.3
  149.9 2.4 pad_maximum_fusion
  152.3 8.2 %multiply_reduce_fusion = (f32[320]{0:T(512)S(1)}, f32[320]{0:T(512)S(1)}, f32[320,512]{1,0:T(8,128)}) fusion(bf16[320,512]{1,0:T(8,128)(2,1)S(1)} %multiply_convert_fusion.2, f32[320,512]{1,0:T(8,128)S(1)} %fusion.7, f32[320,512]{1,0:T(8,128)S(1)} %fusion.11, bf16[320,7168]{1,0:T(8,128)(2,1)} %all-gather.5.cloned.1.call-done, bf16[1,512,7168]{2,1,0:T(8,128)(2,1)} %param.12), kind=kOutput, calls=%fused_computation.46 | convolution fusion | flops 2352414208 | bytes 14223872 | tf_op jit(solution)/shard_map/dot_general | solution.py:82
  160.6 0.3 reduce-scatter.5.cloned.1.call-start
  160.8 0.2 copy.24
  161.0 6.3 %fusion.9 = f32[320,7168]{1,0:T(8,128)S(1)} fusion(bf16[1,7168,512]{2,1,0:T(8,128)(2,1)} %param.10, f32[320,512]{1,0:T(8,128)} %copy-done.3, f32[320,512]{1,0:T(8,128)} %get-tuple-element.38, f32[320,512]{1,0:T(8,128)} %copy-done.4), kind=kOutput, calls=%fused_computation.14 | convolution fusion | flops 2350448640 | bytes 18481152 | tf_op jit(solution)/shard_map/dot_general | solution.py:86
  167.4 8.4 %fusion = bf16[320,7168]{1,0:T(8,128)(2,1)} fusion(f32[320,7168]{1,0:T(8,128)S(1)} %fusion.9, bf16[1,7168,512]{2,1,0:T(8,128)(2,1)} %param.11, f32[320,512]{1,0:T(8,128)} %get-tuple-element.38, f32[320,512]{1,0:T(8,128)} %copy-done.3), kind=kOutput, calls=%fused_computation.1 | convolution fusion | flops 2354380800 | bytes 22413312 | tf_op jit(solution)/shard_map/dot_general | solution.py:87
  175.8 2.6 fusion.13
  178.4 57.6 %all_to_all.22 = bf16[8,40,7296]{2,1,0:T(8,128)(2,1)S(1)} all-to-all(bf16[8,40,7296]{2,1,0:T(8,128)(2,1)S(1)} %bitcast.63), channel_id=1, replica_groups=mesh['region'=8,'local'=4] {'region'}, dimensions={0} | all-to-all | bytes 9338880 | tf_op jit(solution)/shard_map/all_to_all | solution.py:58
  236.0 1.1 fusion.15
  237.1 1.0 copy-done.2
  238.1 1.2 fusion.2
  239.3 0.1 slice_bitcast_fusion.7
  239.4 1.5 pad_maximum_fusion.1
  240.9 1.4 reduce-scatter.3.cloned.1.call-done
  242.3 3.8 %all-to-all-start.3 = ((bf16[8,40,1792]{2,1,0:T(8,128)(2,1)}), bf16[8,40,1792]{2,1,0:T(8,128)(2,1)S(1)}, u32[]{:S(2)}, u32[]{:S(2)}) async-start(bf16[8,40,1792]{2,1,0:T(8,128)(2,1)} %bitcast.74), calls=%async_computation.4 | async-start | bytes 2293760 | tf_op jit(solution)/shard_map/all_to_all | solution.py:58
  246.1 1.1 fusion.30
  247.2 11.4 %psum.7 = f32[128,2,2]{0,2,1:T(2,128)S(1)} all-reduce(f32[128,2,2]{0,2,1:T(2,128)S(1)} %slice_add_fusion), channel_id=1, replica_groups=mesh['region'=8,'local'=4] {'local'}, use_global_device_ids=true, to_apply=%region_9.10 | all-reduce | flops 512 | bytes 4096 | tf_op jit(solution)/shard_map/psum | solution.py:106
  258.7 0.6 fusion.47
  259.3 3.3 %all-to-all-done.3 = bf16[8,40,1792]{2,1,0:T(8,128)(2,1)S(1)} async-done(((bf16[8,40,1792]{2,1,0:T(8,128)(2,1)}), bf16[8,40,1792]{2,1,0:T(8,128)(2,1)S(1)}, u32[]{:S(2)}, u32[]{:S(2)}) %all-to-all-start.3) | async-done | bytes 1146912 | tf_op jit(solution)/shard_map/all_to_all | solution.py:58
  262.6 0.4 fusion.43
  263.0 1.2 fusion.20
  264.2 20.2 %reduce-scatter.5.cloned.1.call-done = bf16[1,128,1792]{2,1,0:T(8,128)(2,1)} async-done(((bf16[4,128,1792]{2,1,0:T(8,128)(2,1)}), bf16[1,128,1792]{2,1,0:T(8,128)(2,1)}) %reduce-scatter.5.cloned.1.call-update) | async-done | bytes 458768 | tf_op jit(solution)/shard_map/reduce_scatter | solution.py:39
  284.4 2.1 fusion.28
  (43 shorter events, 0.3 us)
Async XLA Ops:
  7.2 5.6 %copy-start = (bf16[128,1792]{1,0:T(8,128)(2,1)S(1)}, bf16[128,1792]{1,0:T(8,128)(2,1)}, u32[]{:S(2)}) copy-start(bf16[128,1792]{1,0:T(8,128)(2,1)} %param.15) | copy-start | bytes 1376260
  7.2 48.9 %all-gather.3.cloned.1.call-start = ((), (), s32[]{:S(2)}) async-start(), calls=%async_computation.6 | async-start | bytes 2437120 | tf_op jit(solution)/shard_map/all_gather | solution.py:32
  9.9 133.8 %all-gather.5.cloned.1.call-start = ((), (), s32[]{:S(2)}) async-start(), calls=%async_computation.7 | async-start | bytes 5734400 | tf_op jit(solution)/shard_map/all_gather | solution.py:32
  56.1 186.2 %reduce-scatter.3.cloned.1.call-start = ((), (), s32[]{:S(2)}) async-start(), calls=%async_computation.8 | async-start | bytes 5734400 | tf_op jit(solution)/shard_map/reduce_scatter | solution.py:39
  56.2 63.2 %slice-start.2 = ((s8[7340032]{0:T(1024)(128)(4,1)}), s8[4194304]{0:T(1024)(128)(4,1)S(1)}, s32[]{:S(2)}) async-start(s8[7340032]{0:T(1024)(128)(4,1)} %bitcast.68), calls=%async_computation.12 | async-start | bytes 8388608
  59.2 60.1 %slice-start.3 = ((s8[7340032]{0:T(1024)(128)(4,1)}), s8[3145728]{0:T(1024)(128)(4,1)S(1)}, s32[]{:S(2)}) async-start(s8[7340032]{0:T(1024)(128)(4,1)} %bitcast.68), calls=%async_computation.13 | async-start | bytes 6291456
  62.4 59.5 %slice-start = ((s8[7340032]{0:T(1024)(128)(4,1)}), s8[3145728]{0:T(1024)(128)(4,1)S(1)}, s32[]{:S(2)}) async-start(s8[7340032]{0:T(1024)(128)(4,1)} %bitcast.66), calls=%async_computation.10 | async-start | bytes 6291456
  119.4 2.5 slice-start.1
  121.9 30.4 %copy-start.4 = (f32[320,512]{1,0:T(8,128)}, f32[320,512]{1,0:T(8,128)S(1)}, u32[]{:S(2)}) copy-start(f32[320,512]{1,0:T(8,128)S(1)} %fusion.7) | copy-start | bytes 1966084
  124.5 27.9 %copy-start.3 = (f32[320,512]{1,0:T(8,128)}, f32[320,512]{1,0:T(8,128)S(1)}, u32[]{:S(2)}) copy-start(f32[320,512]{1,0:T(8,128)S(1)} %fusion.11) | copy-start | bytes 1966084
  160.6 123.9 %reduce-scatter.5.cloned.1.call-start = ((), (), s32[]{:S(2)}) async-start(), calls=%async_computation.9 | async-start | bytes 2293760 | tf_op jit(solution)/shard_map/reduce_scatter | solution.py:39
  236.0 2.1 copy-start.2
  239.4 19.8 %copy-start.7 = (f32[128,2]{0,1:T(2,128)S(1)}, f32[128,2]{0,1:T(2,128)}, u32[]{:S(2)}) copy-start(f32[128,2]{0,1:T(2,128)} %param.14) | copy-start | bytes 3076
  242.3 42.2 %copy-start.5 = (bf16[128,1792]{1,0:T(8,128)(2,1)S(1)}, bf16[128,1792]{1,0:T(8,128)(2,1)}, u32[]{:S(2)}) copy-start(bf16[128,1792]{1,0:T(8,128)(2,1)} %param.8) | copy-start | bytes 1376260
  242.3 42.2 %copy-start.6 = (f32[1792]{0:T(1024)S(1)}, f32[1792]{0:T(1024)}, u32[]{:S(2)}) copy-start(f32[1792]{0:T(1024)} %param.9) | copy-start | bytes 21508
  242.3 44.3 %copy-start.1 = (bf16[128,1792]{1,0:T(8,128)(2,1)S(1)}, bf16[128,1792]{1,0:T(8,128)(2,1)}, u32[]{:S(2)}) copy-start(bf16[128,1792]{1,0:T(8,128)(2,1)} %param.15) | copy-start | bytes 1376260
  242.3 20.3 %all-to-all-start.3 = ((bf16[8,40,1792]{2,1,0:T(8,128)(2,1)}), bf16[8,40,1792]{2,1,0:T(8,128)(2,1)S(1)}, u32[]{:S(2)}, u32[]{:S(2)}) async-start(bf16[8,40,1792]{2,1,0:T(8,128)(2,1)} %bitcast.74), calls=%async_computation.4 | async-start | bytes 2293760 | tf_op jit(solution)/shard_map/all_to_all | solution.py:58
Sparse Core Ops, SparseCore 0:
  10.1 45.9 all-gather.2
  57.6 86.0 all-gather.4
  160.7 81.5 reduce-scatter.2
  244.4 39.9 reduce-scatter.4
